TPU v7x, 32 devices: a whole 2x2x4 slice. The times are simulated.
32 devices in a mesh: ctx: 8 (over z, x), wsh: 4 (over y, core).
Axes of the slice: x: 2, y: 2, z: 4, core: 2. Of those that a mesh axis runs over, the one named last changes fastest.
Arguments:
- inputs: bfloat16 [2048, 8, 576], P('ctx', 'wsh'), may hold values from -6 to 6
- query_weight: bfloat16 [576, 576], P('wsh'), may hold values from -0.5 to 0.5
- key_weight: bfloat16 [576, 192], P('wsh'), may hold values from -0.25 to 0.25
- value_weight: bfloat16 [576, 192], P('wsh'), may hold values from -0.25 to 0.25
- output_weight: bfloat16 [576, 576], P('wsh'), may hold values from -1.5 to 1.5
- gate_weight: bfloat16 [576, 1536], P('wsh'), may hold values from -0.25 to 0.25
- up_weight: bfloat16 [576, 1536], P('wsh'), may hold values from -0.25 to 0.25
- down_weight: bfloat16 [1536, 576], P('wsh'), may hold values from -0.15625 to 0.15625
- attn_gain: bfloat16 [576], P('wsh'), may hold values from 0.5 to 1.5
- ffn_gain: bfloat16 [576], P('wsh'), may hold values from 0.5 to 1.5
- cotangent: bfloat16 [2048, 8, 576], P('ctx', 'wsh'), may hold values from -6 to 6
Outputs:
- layer_out: bfloat16 [2048, 8, 576], P('ctx', 'wsh')
- input_grad: bfloat16 [2048, 8, 576], P('ctx', 'wsh')
- query_grad: float32 [576, 576], P('wsh')
- key_grad: float32 [576, 192], P('wsh')
- value_grad: float32 [576, 192], P('wsh')
- project_grad: float32 [576, 576], P('wsh')
- gate_grad: float32 [576, 1536], P('wsh')
- up_grad: float32 [576, 1536], P('wsh')
- down_grad: float32 [1536, 576], P('wsh')
- attn_gain_grad: float32 [576], P('wsh')
- ffn_gain_grad: float32 [576], P('wsh')
All inputs are finite; a program needn't handle non-finite values.
Results may differ from a plain program's by a relative error of at most 0.017.
The roundings to bfloat16 on the way count: a program that leaves them out, or rounds other values in their place, can miss the bound.
Values may be sent and summed in bfloat16 or wider, within the bound.
A program may use at most 256 MiB of HBM per device.

v0:
```python
import math

import jax
import jax.numpy as jnp
from jax import lax
from jax.sharding import PartitionSpec as P

D = 576
HEADS = 9
KV_HEADS = 3
HEAD = 64


epsilon = 1e-05
rope_base = 100000.0


def rms_norm(values, gain):
    factor = lax.rsqrt(jnp.mean(values * values, axis=-1, keepdims=True) + epsilon)
    return values * factor * gain


def rope_tables(positions):
    half = HEAD // 2
    rates = rope_base ** (-(2.0 * jnp.arange(half, dtype=jnp.float32)) / HEAD)
    angles = positions[:, None] * rates[None, :]
    return (jnp.cos(angles), jnp.sin(angles))


def rotate(values, cosine, sine):
    half = values.shape[-1] // 2
    first = values[..., :half]
    second = values[..., half:]
    cosine = cosine[:, None, :]
    sine = sine[:, None, :]
    return jnp.concatenate(
        [first * cosine - second * sine, second * cosine + first * sine], axis=-1
    )


def sweep(state, pairs, last_query, step):
    length = pairs.shape[0]
    width = math.gcd(length, 1024)
    count = length // width
    upper = jnp.clip(last_query // width + 1, 0, count)

    def advance(index, carry):
        begin = index * width
        piece = lax.dynamic_slice_in_dim(pairs, begin, width, 0)
        return step(carry, piece, begin)

    return lax.fori_loop(0, upper, advance, state)


def local(
    inputs,
    query_weight,
    key_weight,
    value_weight,
    output_weight,
    gate_weight,
    up_weight,
    down_weight,
    attn_gain,
    ffn_gain,
    cotangent,
):
    gathered = (
        lax.all_gather(query_weight, "wsh", axis=0, tiled=True),
        lax.all_gather(key_weight, "wsh", axis=0, tiled=True),
        lax.all_gather(value_weight, "wsh", axis=0, tiled=True),
        lax.all_gather(output_weight, "wsh", axis=0, tiled=True),
        lax.all_gather(gate_weight, "wsh", axis=0, tiled=True),
        lax.all_gather(up_weight, "wsh", axis=0, tiled=True),
        lax.all_gather(down_weight, "wsh", axis=0, tiled=True),
        lax.all_gather(attn_gain, "wsh", axis=0, tiled=True),
        lax.all_gather(ffn_gain, "wsh", axis=0, tiled=True),
    )
    w_query, w_key, w_value, w_out, w_gate, w_up, w_down, gain_first, gain_second = gathered
    gain_first = gain_first.astype(jnp.float32)
    gain_second = gain_second.astype(jnp.float32)
    tokens = inputs.shape[0]
    batch = inputs.shape[1]
    rows = tokens * batch
    per_group = HEADS // KV_HEADS
    pair_width = KV_HEADS * HEAD
    scale = HEAD ** (-0.5)
    cycle_index = lax.axis_index("ctx")
    cycle_size = lax.axis_size("ctx")
    start_pos = cycle_index * tokens
    last_query = start_pos + tokens - 1
    query_pos = start_pos + jnp.arange(tokens, dtype=jnp.int32)
    cosine, sine = rope_tables(query_pos.astype(jnp.float32))
    full_length = cycle_size * tokens
    residual = inputs.reshape(rows, D).astype(jnp.float32)
    normed = rms_norm(residual, gain_first).astype(jnp.bfloat16)
    query_pre = jnp.dot(normed, w_query, preferred_element_type=jnp.float32)
    key_pre = jnp.dot(normed, w_key, preferred_element_type=jnp.float32)
    value_pre = jnp.dot(normed, w_value, preferred_element_type=jnp.float32)
    queries = (
        rotate(query_pre.reshape(tokens, batch * HEADS, HEAD), cosine, sine)
        .astype(jnp.bfloat16)
        .reshape(tokens, batch, KV_HEADS, per_group, HEAD)
    )
    keys = (
        rotate(key_pre.reshape(tokens, batch * KV_HEADS, HEAD), cosine, sine)
        .astype(jnp.bfloat16)
        .reshape(tokens, batch, pair_width)
    )
    pairs = jnp.concatenate(
        [keys, value_pre.astype(jnp.bfloat16).reshape(tokens, batch, pair_width)], axis=-1
    )

    def split_pairs(piece):
        count = piece.shape[0]
        return (
            piece[..., :pair_width].reshape(count, batch, KV_HEADS, HEAD),
            piece[..., pair_width:].reshape(count, batch, KV_HEADS, HEAD),
        )

    def exponents(piece_keys, first):
        scores = (
            jnp.einsum("qsgrd,ksgd->sgrqk", queries, piece_keys, preferred_element_type=jnp.float32)
            * scale
        )
        key_pos = first + jnp.arange(piece_keys.shape[0], dtype=jnp.int32)
        causal = query_pos[:, None] >= key_pos[None, :]
        return jnp.where(causal, jnp.exp(scores), 0.0)

    def forward_step(state, piece, first):
        weighted, total = state
        piece_keys, piece_values = split_pairs(piece)
        powers = exponents(piece_keys, first)
        weighted = weighted + jnp.einsum(
            "sgrqk,ksgd->qsgrd",
            powers.astype(jnp.bfloat16),
            piece_values,
            preferred_element_type=jnp.float32,
        )
        return (weighted, total + jnp.sum(powers, axis=-1))

    start_state = (
        jnp.zeros((tokens, batch, KV_HEADS, per_group, HEAD), jnp.float32),
        jnp.zeros((batch, KV_HEADS, per_group, tokens), jnp.float32),
    )
    weighted, total = sweep(
        start_state, lax.all_gather(pairs, "ctx", axis=0, tiled=True), last_query, forward_step
    )
    totals_moved = jnp.transpose(total, (3, 0, 1, 2))[..., None]
    mixed = weighted / totals_moved
    mixed_low = mixed.astype(jnp.bfloat16).reshape(rows, D)
    middle = residual + jnp.dot(mixed_low, w_out, preferred_element_type=jnp.float32)
    normed_two = rms_norm(middle, gain_second).astype(jnp.bfloat16)
    gate = jnp.dot(normed_two, w_gate, preferred_element_type=jnp.float32)
    up = jnp.dot(normed_two, w_up, preferred_element_type=jnp.float32)
    hidden = (jax.nn.silu(gate) * up).astype(jnp.bfloat16)
    result = middle + jnp.dot(hidden, w_down, preferred_element_type=jnp.float32)
    layer_out = result.astype(jnp.bfloat16).reshape(tokens, batch, D)
    seed = cotangent.reshape(rows, D)
    grad_down = jnp.einsum("nf,nd->fd", hidden, seed, preferred_element_type=jnp.float32)
    grad_hidden = jnp.einsum("nd,fd->nf", seed, w_down, preferred_element_type=jnp.float32)
    unused_value, swiglu_back = jax.vjp(lambda left, right: jax.nn.silu(left) * right, gate, up)
    grad_gate_f, grad_up_f = swiglu_back(grad_hidden)
    gate_back = grad_gate_f.astype(jnp.bfloat16)
    up_back = grad_up_f.astype(jnp.bfloat16)
    grad_wgate = jnp.einsum("nd,nf->df", normed_two, gate_back, preferred_element_type=jnp.float32)
    grad_wup = jnp.einsum("nd,nf->df", normed_two, up_back, preferred_element_type=jnp.float32)
    grad_normed_two = jnp.einsum(
        "nf,df->nd", gate_back, w_gate, preferred_element_type=jnp.float32
    ) + jnp.einsum("nf,df->nd", up_back, w_up, preferred_element_type=jnp.float32)
    unused_norm, second_norm_back = jax.vjp(rms_norm, middle, gain_second)
    grad_middle_norm, grad_gain_second = second_norm_back(grad_normed_two)
    grad_middle = seed.astype(jnp.float32) + grad_middle_norm
    attn_seed = grad_middle.astype(jnp.bfloat16)
    grad_project = jnp.einsum("nd,ne->de", mixed_low, attn_seed, preferred_element_type=jnp.float32)
    grad_mixed = jnp.einsum(
        "ne,de->nd", attn_seed, w_out, preferred_element_type=jnp.float32
    ).reshape(tokens, batch, KV_HEADS, per_group, HEAD)
    scaled = (grad_mixed / totals_moved).astype(jnp.bfloat16)
    offset = jnp.sum(grad_mixed * mixed, axis=-1) / totals_moved[..., 0]
    offset_moved = jnp.transpose(offset, (1, 2, 3, 0))[..., None]

    def backward_step(state, piece, first):
        grad_queries, grad_pairs = state
        piece_keys, piece_values = split_pairs(piece)
        powers = exponents(piece_keys, first)
        inner = jnp.einsum(
            "qsgrd,ksgd->sgrqk", scaled, piece_values, preferred_element_type=jnp.float32
        )
        grad_scores = (powers * (inner - offset_moved)).astype(jnp.bfloat16)
        grad_queries = (
            grad_queries
            + jnp.einsum(
                "sgrqk,ksgd->qsgrd", grad_scores, piece_keys, preferred_element_type=jnp.float32
            )
            * scale
        )
        grad_keys = (
            jnp.einsum(
                "sgrqk,qsgrd->ksgd", grad_scores, queries, preferred_element_type=jnp.float32
            )
            * scale
        )
        grad_values = jnp.einsum(
            "sgrqk,qsgrd->ksgd",
            powers.astype(jnp.bfloat16),
            scaled,
            preferred_element_type=jnp.float32,
        )
        count = piece.shape[0]
        term = jnp.concatenate(
            [
                grad_keys.reshape(count, batch, pair_width),
                grad_values.reshape(count, batch, pair_width),
            ],
            axis=-1,
        )
        return (grad_queries, lax.dynamic_update_slice_in_dim(grad_pairs, term, first, 0))

    back_state = (
        jnp.zeros((tokens, batch, KV_HEADS, per_group, HEAD), jnp.float32),
        jnp.zeros((full_length, batch, 2 * pair_width), jnp.float32),
    )
    grad_queries, grad_pairs = sweep(
        back_state, lax.all_gather(pairs, "ctx", axis=0, tiled=True), last_query, backward_step
    )
    own_pairs = lax.psum_scatter(grad_pairs, "ctx", scatter_dimension=0, tiled=True)
    query_back = (
        rotate(grad_queries.reshape(tokens, batch * HEADS, HEAD), cosine, -sine)
        .astype(jnp.bfloat16)
        .reshape(rows, D)
    )
    key_back = (
        rotate(own_pairs[..., :pair_width].reshape(tokens, batch * KV_HEADS, HEAD), cosine, -sine)
        .astype(jnp.bfloat16)
        .reshape(rows, pair_width)
    )
    value_back = own_pairs[..., pair_width:].astype(jnp.bfloat16).reshape(rows, pair_width)
    grad_wquery = jnp.einsum("nd,nk->dk", normed, query_back, preferred_element_type=jnp.float32)
    grad_wkey = jnp.einsum("nd,nk->dk", normed, key_back, preferred_element_type=jnp.float32)
    grad_wvalue = jnp.einsum("nd,nk->dk", normed, value_back, preferred_element_type=jnp.float32)
    grad_normed = jnp.einsum("nk,dk->nd", query_back, w_query, preferred_element_type=jnp.float32)
    grad_normed = grad_normed + jnp.einsum(
        "nk,dk->nd", key_back, w_key, preferred_element_type=jnp.float32
    )
    grad_normed = grad_normed + jnp.einsum(
        "nk,dk->nd", value_back, w_value, preferred_element_type=jnp.float32
    )
    unused_first, first_norm_back = jax.vjp(rms_norm, residual, gain_first)
    grad_residual, grad_gain_first = first_norm_back(grad_normed)
    input_grad = (grad_middle + grad_residual).astype(jnp.bfloat16).reshape(tokens, batch, D)
    shares = (
        lax.psum_scatter(grad_wquery, "wsh", scatter_dimension=0, tiled=True),
        lax.psum_scatter(grad_wkey, "wsh", scatter_dimension=0, tiled=True),
        lax.psum_scatter(grad_wvalue, "wsh", scatter_dimension=0, tiled=True),
        lax.psum_scatter(grad_project, "wsh", scatter_dimension=0, tiled=True),
        lax.psum_scatter(grad_wgate, "wsh", scatter_dimension=0, tiled=True),
        lax.psum_scatter(grad_wup, "wsh", scatter_dimension=0, tiled=True),
        lax.psum_scatter(grad_down, "wsh", scatter_dimension=0, tiled=True),
        lax.psum_scatter(grad_gain_first, "wsh", scatter_dimension=0, tiled=True),
        lax.psum_scatter(grad_gain_second, "wsh", scatter_dimension=0, tiled=True),
    )
    owned = lax.psum(
        (
            shares[0],
            shares[1],
            shares[2],
            shares[3],
            shares[4],
            shares[5],
            shares[6],
            shares[7],
            shares[8],
        ),
        "ctx",
    )
    return (
        layer_out,
        input_grad,
        owned[0],
        owned[1],
        owned[2],
        owned[3],
        owned[4],
        owned[5],
        owned[6],
        owned[7],
        owned[8],
    )


def solution(mesh):
    in_specs = (
        P("ctx", "wsh", None),
        P("wsh", None),
        P("wsh", None),
        P("wsh", None),
        P("wsh", None),
        P("wsh", None),
        P("wsh", None),
        P("wsh", None),
        P("wsh"),
        P("wsh"),
        P("ctx", "wsh", None),
    )
    out_specs = (
        P("ctx", "wsh", None),
        P("ctx", "wsh", None),
        P("wsh", None),
        P("wsh", None),
        P("wsh", None),
        P("wsh", None),
        P("wsh", None),
        P("wsh", None),
        P("wsh", None),
        P("wsh"),
        P("wsh"),
    )
    return jax.shard_map(local, mesh=mesh, in_specs=in_specs, out_specs=out_specs, check_vma=False)
```

profile of v0, /device:TPU:0, one launch (start us, length us, event | category | flops | bytes accessed | tf_op | source)
XLA Modules:
  0.0 802.3 jit_solution(18396807025664056322)
XLA Ops:
  12.8 8.3 %all-reduce.7 = (bf16[576]{0:T(1024)(128)(2,1)S(1)}, bf16[576]{0:T(1024)(128)(2,1)S(1)}) all-reduce(bf16[576]{0:T(1024)(128)(2,1)S(1)} %dynamic-update-slice, bf16[576]{0:T(1024)(128)(2,1)S(1)} %dynamic-update-slice.1), channel_id=1, replica_groups=mesh['ctx'=8,'wsh'=4] {'wsh'}, use_global_device_ids=true, to_apply=%add | all-reduce | flops 1152 | bytes 4608
  22.1 5.9 all_gather.32
  27.9 6.0 all_gather.33
  46.2 8.4 %all_gather.35 = bf16[576,576]{1,0:T(8,128)(2,1)S(1)} all-gather(bf16[144,576]{1,0:T(8,128)(2,1)S(1)} %copy-done.48), channel_id=1, replica_groups=mesh['ctx'=8,'wsh'=4] {'wsh'}, dimensions={0}, use_global_device_ids=true | all-gather | bytes 829440 | tf_op jit(solution)/shard_map/all_gather | solution.py:69
  54.6 9.4 %all_gather.36 = bf16[576,576]{1,0:T(8,128)(2,1)} all-gather(bf16[144,576]{1,0:T(8,128)(2,1)S(1)} %copy-done.49), channel_id=1, replica_groups=mesh['ctx'=8,'wsh'=4] {'wsh'}, dimensions={0}, use_global_device_ids=true | all-gather | bytes 829440 | tf_op jit(solution)/shard_map/all_gather | solution.py:72
  73.8 31.1 %all-gather.5.cloned.1.call-done = bf16[2048,2,384]{0,2,1:T(8,128)(2,1)} async-done(((bf16[256,2,384]{0,2,1:T(8,128)(2,1)}), bf16[2048,2,384]{0,2,1:T(8,128)(2,1)}) %all-gather.5.cloned.1.call-update) | async-done | bytes 3145744 | tf_op jit(solution)/shard_map/all_gather | solution.py:147
  105.0 9.7 %while.26 = (s32[]{:T(128)}, f32[256,2,3,3,64]{0,4,3,2,1:T(8,128)S(1)}, f32[2,3,3,256]{3,2,1,0:T(4,128)S(1)}, s32[]{:T(128)}, bf16[2048,2,384]{0,2,1:T(8,128)(2,...) while((s32[]{:T(128)}, ...), condition=%wide.region_3.4_spmd.clone, body=%wide.region_1.3_spmd.clone.sunk | while | flops 1236829440 | bytes 46287040 | solution.py:52
  120.3 4.9 fusion.43
  130.3 4.8 fusion.52
  135.1 12.8 %all-gather.7.cloned.1.call-done = bf16[576,1536]{1,0:T(8,128)(2,1)} async-done(((bf16[144,1536]{1,0:T(8,128)(2,1)}), bf16[576,1536]{1,0:T(8,128)(2,1)}) %all-gather.7.cloned.1.call-update) | async-done | bytes 1769488 | tf_op jit(solution)/shard_map/all_gather | solution.py:73
  147.9 4.6 fusion.51
  152.5 17.6 %all-gather.11.cloned.1.call-done = bf16[1536,576]{0,1:T(8,128)(2,1)} async-done(((bf16[384,576]{0,1:T(8,128)(2,1)}), bf16[1536,576]{0,1:T(8,128)(2,1)}) %all-gather.11.cloned.1.call-update) | async-done | bytes 1769488 | tf_op jit(solution)/shard_map/all_gather | solution.py:75
  170.1 5.8 multiply_convert_fusion
  184.2 4.4 reshape.281
  188.5 6.3 multiply_reduce_fusion
  203.4 37.4 %while.27 = (s32[]{:T(128)}, f32[256,2,3,3,64]{0,4,3,2,1:T(8,128)S(1)}, f32[2048,2,384]{0,2,1:T(8,128)}, s32[]{:T(128)}, bf16[2048,2,384]{0,2,1:T(8,128)(2,1)}, ...) while((s32[]{:T(128)}, ...), condition=%wide.region_8.9_spmd.clone, body=%wide.region_7.8_spmd.clone.sunk | while | flops 3059680512 | bytes 111702264 | solution.py:52
  206.1 7.9 fusion.147
  213.9 10.8 %fusion.150 = f32[2,3,1024,64,1]{2,3,4,1,0:T(8,128)} fusion(bf16[256,2,3,3,64]{0,4,3,2,1:T(8,128)(2,1)} %get-tuple-element.486, f32[2,3,1024,256,3]{3,2,4,1,0:T(8,128)} %fusion.147, pred[256,1024]{0,1:T(8,128)(4,1)} %broadcast_compare_fusion.5), kind=kOutput, calls=%fused_computation.21.clone.1 | convolution fusion | flops 618135552 | bytes 21299200 | tf_op jit(solution)/shard_map/while/body/sgrqk,qsgrd->ksgd/dot_general | solution.py:204
  224.7 9.1 %fusion.148 = bf16[2,3,3,256,1024]{3,4,2,1,0:T(8,128)(2,1)S(1)} fusion(f32[2,3,1024,256,3]{3,2,4,1,0:T(8,128)} %fusion.147, f32[2,3,3,256]{3,2,1,0:T(4,128)S(1)} %bitcast.199, pred[256,1024]{0,1:T(8,128)(4,1)} %broadcast_compare_fusion.5, bf16[1024,2,3,64,1]{0,3,4,2,1:T(8,128)(2,1)S(1)} %bitcast.193, bf16[256,2,3,3,64]{0,4,3,2,1:T(8,128)(2,1)} %get-tuple-element.486), kind=kOutput, calls=%fused_computation.18.clone.1 | convolution fusion | flops 627572736 | bytes 29968384 | tf_op jit(solution)/shard_map/while/body/qsgrd,ksgd->sgrqk/dot_general | solution.py:187
  254.1 4.4 multiply_subtract_fusion
  274.9 4.4 fusion.59
  279.4 117.1 %reduce-scatter.9.cloned.1.call-done = f32[256,2,384]{0,2,1:T(8,128)} async-done(((f32[2048,2,384]{0,2,1:T(8,128)}), f32[256,2,384]{0,2,1:T(8,128)}) %reduce-scatter.9.cloned.1.call-update) | async-done | bytes 786448 | tf_op jit(solution)/shard_map/reduce_scatter | solution.py:227
  406.6 19.1 %reduce-scatter.17.cloned.1.call-done = f32[144,576]{1,0:T(8,128)} async-done(((f32[576,576]{1,0:T(8,128)}), f32[144,576]{1,0:T(8,128)}) %reduce-scatter.17.cloned.1.call-update) | async-done | bytes 331792 | tf_op jit(solution)/shard_map/reduce_scatter | solution.py:256
  425.7 30.3 %reduce-scatter.11.cloned.1.call-done = f32[144,576]{1,0:T(8,128)} async-done(((f32[576,576]{1,0:T(8,128)}), f32[144,576]{1,0:T(8,128)}) %reduce-scatter.11.cloned.1.call-update) | async-done | bytes 331792 | tf_op jit(solution)/shard_map/reduce_scatter | solution.py:253
  456.0 43.0 %reduce-scatter.21.cloned.1.call-done = f32[144,1536]{1,0:T(8,128)} async-done(((f32[576,1536]{1,0:T(8,128)}), f32[144,1536]{1,0:T(8,128)}) %reduce-scatter.21.cloned.1.call-update) | async-done | bytes 884752 | tf_op jit(solution)/shard_map/reduce_scatter | solution.py:258
  499.0 43.2 %reduce-scatter.19.cloned.1.call-done = f32[144,1536]{1,0:T(8,128)} async-done(((f32[576,1536]{1,0:T(8,128)}), f32[144,1536]{1,0:T(8,128)}) %reduce-scatter.19.cloned.1.call-update) | async-done | bytes 884752 | tf_op jit(solution)/shard_map/reduce_scatter | solution.py:257
  542.2 42.9 %reduce-scatter.23.cloned.1.call-done = f32[384,576]{0,1:T(8,128)} async-done(((f32[1536,576]{0,1:T(8,128)}), f32[384,576]{0,1:T(8,128)}) %reduce-scatter.23.cloned.1.call-update) | async-done | bytes 884752 | tf_op jit(solution)/shard_map/reduce_scatter | solution.py:259
  585.1 25.3 %reduce-scatter.15.cloned.1.call-done = f32[144,192]{1,0:T(8,128)} async-done(((f32[576,192]{1,0:T(8,128)}), f32[144,192]{1,0:T(8,128)}) %reduce-scatter.15.cloned.1.call-update) | async-done | bytes 110608 | tf_op jit(solution)/shard_map/reduce_scatter | solution.py:255
  610.4 25.2 %reduce-scatter.13.cloned.1.call-done = f32[144,192]{1,0:T(8,128)} async-done(((f32[576,192]{1,0:T(8,128)}), f32[144,192]{1,0:T(8,128)}) %reduce-scatter.13.cloned.1.call-update) | async-done | bytes 110608 | tf_op jit(solution)/shard_map/reduce_scatter | solution.py:254
  647.3 6.8 all-reduce.6
  661.7 23.3 %all-reduce.4 = (f32[144]{0:T(256)}, f32[144]{0:T(256)}) all-reduce(f32[144]{0:T(256)S(1)} %dynamic-slice.3, f32[144]{0:T(256)S(1)} %copy-done.59), channel_id=1, replica_groups=mesh['ctx'=8,'wsh'=4] {'ctx'}, use_global_device_ids=true, to_apply=%region_27.28 | all-reduce | flops 288 | bytes 2304 | tf_op jit(solution)/shard_map/psum | solution.py:263
  685.0 102.0 %all-reduce.10.cloned.1.call-done = (f32[144,576]{1,0:T(8,128)}, f32[144,192]{1,0:T(8,128)}, f32[144,192]{1,0:T(8,128)}, f32[144,576]{1,0:T(8,128)}, f32[144,153...) async-done(((f32[144,576]{1,0:T(8,128)}, f32[144,192]{1,0:T(8,128)}, f32[144,192]{1,0:T(8,128)}, f32[144,576]{1,0:T(8,128)}, f32[144,1536]{1,0:T(8,128)}, ...) | async-done | bytes 3538960 | tf_op jit(solution)/shard_map/psum | solution.py:263
  (281 shorter events, 140.3 us)
Async XLA Ops:
  7.2 14.8 %copy-start.52 = (bf16[144,192]{1,0:T(8,128)(2,1)S(1)}, bf16[144,192]{1,0:T(8,128)(2,1)}, u32[]{:S(2)}) copy-start(bf16[144,192]{1,0:T(8,128)(2,1)} %param.17) | copy-start | bytes 165892
  7.2 97.7 %all-gather.5.cloned.1.call-start = ((), (), s32[]{:S(2)}) async-start(), calls=%async_computation.8 | async-start | bytes 3538944 | tf_op jit(solution)/shard_map/all_gather | solution.py:147
  7.3 20.6 %copy-start.53 = (bf16[144,192]{1,0:T(8,128)(2,1)S(1)}, bf16[144,192]{1,0:T(8,128)(2,1)}, u32[]{:S(2)}) copy-start(bf16[144,192]{1,0:T(8,128)(2,1)} %param.18) | copy-start | bytes 165892
  21.1 14.1 %copy-start.50 = (f32[576]{0:T(1024)}, f32[576]{0:T(1024)S(1)}, u32[]{:S(2)}) copy-start(f32[576]{0:T(1024)S(1)} %convert_element_type.116) | copy-start | bytes 6916
  22.0 5.9 copy-start.56
  22.0 13.2 %copy-start.54 = (f32[512]{0:T(512)}, f32[512]{0:T(512)S(1)}, u32[]{:S(2)}) copy-start(f32[512]{0:T(512)S(1)} %rsqrt.25) | copy-start | bytes 6148
  27.9 9.4 %copy-start.33 = (bf16[576,192]{1,0:T(8,128)(2,1)}, bf16[576,192]{1,0:T(8,128)(2,1)S(1)}, u32[]{:S(2)}) copy-start(bf16[576,192]{1,0:T(8,128)(2,1)S(1)} %all_gather.32) | copy-start | bytes 663556
  39.1 29.2 %copy-start.29 = (f32[256,32]{1,0:T(8,128)}, f32[256,32]{1,0:T(8,128)S(1)}, u32[]{:S(2)}) copy-start(f32[256,32]{1,0:T(8,128)S(1)} %get-tuple-element.297) | copy-start | bytes 98308
  41.4 89.0 %all-gather.9.cloned.1.call-start = ((), (), s32[]{:S(2)}) async-start(), calls=%async_computation.10 | async-start | bytes 2211840 | tf_op jit(solution)/shard_map/all_gather | solution.py:74
  42.1 105.8 %all-gather.7.cloned.1.call-start = ((), (), s32[]{:S(2)}) async-start(), calls=%async_computation.9 | async-start | bytes 2211840 | tf_op jit(solution)/shard_map/all_gather | solution.py:73
  42.8 127.2 %all-gather.11.cloned.1.call-start = ((), (), s32[]{:S(2)}) async-start(), calls=%async_computation.11 | async-start | bytes 2211840 | tf_op jit(solution)/shard_map/all_gather | solution.py:75
  43.4 353.1 %reduce-scatter.9.cloned.1.call-start = ((), (), s32[]{:S(2)}) async-start(), calls=%async_computation.12 | async-start | bytes 7077888 | tf_op jit(solution)/shard_map/reduce_scatter | solution.py:227
  44.6 10.0 %copy-start.49 = (bf16[144,576]{1,0:T(8,128)(2,1)S(1)}, bf16[144,576]{1,0:T(8,128)(2,1)}, u32[]{:S(2)}) copy-start(bf16[144,576]{1,0:T(8,128)(2,1)} %param.19) | copy-start | bytes 497668
  45.1 18.9 %copy-start.19 = (bf16[512,576]{1,0:T(8,128)(2,1)}, bf16[512,576]{1,0:T(8,128)(2,1)S(1)}, u32[]{:S(2)}) copy-start(bf16[512,576]{1,0:T(8,128)(2,1)S(1)} %reshape.280) | copy-start | bytes 1769476
  54.6 9.4 %copy-start.13 = (bf16[576,576]{1,0:T(8,128)(2,1)}, bf16[576,576]{1,0:T(8,128)(2,1)S(1)}, u32[]{:S(2)}) copy-start(bf16[576,576]{1,0:T(8,128)(2,1)S(1)} %all_gather.35) | copy-start | bytes 1990660
  130.3 17.6 %copy-start.11 = (bf16[512,576]{0,1:T(8,128)(2,1)}, bf16[512,576]{0,1:T(8,128)(2,1)S(1)}, u32[]{:S(2)}) copy-start(bf16[512,576]{0,1:T(8,128)(2,1)S(1)} %multiply_convert_fusion.3) | copy-start | bytes 1769476
  135.1 35.0 %copy-start.20 = (bf16[512,576]{1,0:T(8,128)(2,1)S(1)}, bf16[512,576]{1,0:T(8,128)(2,1)}, u32[]{:S(2)}) copy-start(bf16[512,576]{1,0:T(8,128)(2,1)} %copy-done.19) | copy-start | bytes 1769476
  170.1 5.8 copy-start.62
  188.5 6.3 copy-start.28
  240.8 184.8 %reduce-scatter.17.cloned.1.call-start = ((), (), s32[]{:S(2)}) async-start(), calls=%async_computation.16 | async-start | bytes 1843200 | tf_op jit(solution)/shard_map/reduce_scatter | solution.py:256
  244.1 211.8 %reduce-scatter.11.cloned.1.call-start = ((), (), s32[]{:S(2)}) async-start(), calls=%async_computation.13 | async-start | bytes 1843200 | tf_op jit(solution)/shard_map/reduce_scatter | solution.py:253
  265.2 233.8 %reduce-scatter.21.cloned.1.call-start = ((), (), s32[]{:S(2)}) async-start(), calls=%async_computation.18 | async-start | bytes 4423680 | tf_op jit(solution)/shard_map/reduce_scatter | solution.py:258
  269.5 272.7 %reduce-scatter.19.cloned.1.call-start = ((), (), s32[]{:S(2)}) async-start(), calls=%async_computation.17 | async-start | bytes 4423680 | tf_op jit(solution)/shard_map/reduce_scatter | solution.py:257
  273.8 311.2 %reduce-scatter.23.cloned.1.call-start = ((), (), s32[]{:S(2)}) async-start(), calls=%async_computation.19 | async-start | bytes 4423680 | tf_op jit(solution)/shard_map/reduce_scatter | solution.py:259
  279.3 117.2 %copy-start.26 = (bf16[256,2,576]{0,2,1:T(8,128)(2,1)S(1)}, bf16[256,2,576]{0,2,1:T(8,128)(2,1)}, u32[]{:S(2)}) copy-start(bf16[256,2,576]{0,2,1:T(8,128)(2,1)} %copy-done.25) | copy-start | bytes 1769476
  279.3 331.1 %reduce-scatter.15.cloned.1.call-start = ((), (), s32[]{:S(2)}) async-start(), calls=%async_computation.15 | async-start | bytes 737280 | tf_op jit(solution)/shard_map/reduce_scatter | solution.py:255
  398.7 236.9 %reduce-scatter.13.cloned.1.call-start = ((), (), s32[]{:S(2)}) async-start(), calls=%async_computation.14 | async-start | bytes 737280 | tf_op jit(solution)/shard_map/reduce_scatter | solution.py:254
  405.2 230.4 %copy-start.35 = (bf16[512,192]{1,0:T(8,128)(2,1)}, bf16[512,192]{1,0:T(8,128)(2,1)S(1)}, u32[]{:S(2)}) copy-start(bf16[512,192]{1,0:T(8,128)(2,1)S(1)} %convert_element_type.134) | copy-start | bytes 589828
  406.4 380.6 %all-reduce.10.cloned.1.call-start = ((), (), s32[]{:S(2)}) async-start(), calls=%async_computation.20 | async-start | bytes 7372800 | tf_op jit(solution)/shard_map/psum | solution.py:263
  646.3 10.0 %copy-start.57 = (f32[512]{0:T(512)S(1)}, f32[512]{0:T(512)}, u32[]{:S(2)}) copy-start(f32[512]{0:T(512)} %copy-done.56) | copy-start | bytes 6148
  646.3 10.7 %copy-start.6 = (f32[512,576]{0,1:T(8,128)S(1)}, f32[512,576]{0,1:T(8,128)}, u32[]{:S(2)}) copy-start(f32[512,576]{0,1:T(8,128)} %copy-done.4) | copy-start | bytes 3538948
  787.0 5.8 copy-start.44
  (47 other events, 109.6 us)
Sparse Core Ops, SparseCore 0:
  41.5 63.4 all-gather.4
  106.5 19.0 all-gather.8
  127.1 20.7 all-gather.6
  149.3 20.7 all-gather.10
  240.9 155.5 reduce-scatter.8
  398.9 26.7 reduce-scatter.16
  428.4 27.4 reduce-scatter.10
  458.5 40.4 reduce-scatter.20
  501.7 40.4 reduce-scatter.18
  544.6 40.4 reduce-scatter.22
  588.3 22.0 reduce-scatter.14
  613.5 22.0 reduce-scatter.12
  640.8 146.1 all-reduce.9
where the time goes:
time: 810 us; the launch traced here: 802 us
  waiting for transfers between devices  512 us (63%)
  matrix products  90 us (11%)
  local copies, waits for them, and re-layouts  82.2 us (10%)
  blocking collectives  68.2 us (8%)
  other arithmetic  32.2 us (4%)
  between operations  16.4 us (2%)
    reduce_scatter x1, waiting for transfers between devices, local(): lax.psum_scatter(grad_pairs, 'ctx', scatter_dimension=0, tiled=True)  117 us
    psum x1, waiting for transfers between devices, local(): lax.psum((shares[0], shares[1], shares[2], shares[3], shares[4], shares[5...  102 us
    reduce_scatter x1, waiting for transfers between devices, local(): lax.psum_scatter(grad_wgate, 'wsh', scatter_dimension=0, tiled=True)  43.2 us
    reduce_scatter x1, waiting for transfers between devices, local(): lax.psum_scatter(grad_wup, 'wsh', scatter_dimension=0, tiled=True)  43 us
    reduce_scatter x1, waiting for transfers between devices, local(): lax.psum_scatter(grad_down, 'wsh', scatter_dimension=0, tiled=True)  42.9 us
    unnamed x151, local copies, waits for them, and re-layouts  36.2 us
    all_gather x1, waiting for transfers between devices, local(): lax.all_gather(pairs, 'ctx', axis=0, tiled=True)  31.1 us
    reduce_scatter x1, waiting for transfers between devices, local(): lax.psum_scatter(grad_wquery, 'wsh', scatter_dimension=0, tiled=True)  30.3 us
  transfers between devices with their start and end apart: 13, of which 12 were waited for; matrix products, arithmetic and copies ran while one was open for 13% of the time, Pallas kernels for 0%

commit v1 on v0

--- a/solution.py
+++ b/solution.py
@@ -65,18 +65,22 @@
     ffn_gain,
     cotangent,
 ):
-    gathered = (
-        lax.all_gather(query_weight, "wsh", axis=0, tiled=True),
-        lax.all_gather(key_weight, "wsh", axis=0, tiled=True),
-        lax.all_gather(value_weight, "wsh", axis=0, tiled=True),
-        lax.all_gather(output_weight, "wsh", axis=0, tiled=True),
-        lax.all_gather(gate_weight, "wsh", axis=0, tiled=True),
-        lax.all_gather(up_weight, "wsh", axis=0, tiled=True),
-        lax.all_gather(down_weight, "wsh", axis=0, tiled=True),
-        lax.all_gather(attn_gain, "wsh", axis=0, tiled=True),
-        lax.all_gather(ffn_gain, "wsh", axis=0, tiled=True),
-    )
-    w_query, w_key, w_value, w_out, w_gate, w_up, w_down, gain_first, gain_second = gathered
+    first_pack = jnp.concatenate(
+        [query_weight, key_weight, value_weight, attn_gain[:, None], ffn_gain[:, None]], axis=1
+    )
+    first_all = lax.all_gather(first_pack, "wsh", axis=0, tiled=True)
+    w_first = first_all[:, : D + 2 * KV_HEADS * HEAD]
+    gain_first = first_all[:, D + 2 * KV_HEADS * HEAD]
+    gain_second = first_all[:, D + 2 * KV_HEADS * HEAD + 1]
+    width = gate_weight.shape[1]
+    middle_pack = jnp.concatenate([output_weight, gate_weight, up_weight], axis=1)
+    middle_pack, down_weight, first_all = lax.optimization_barrier(
+        (middle_pack, down_weight, first_all)
+    )
+    middle_all = lax.all_gather(middle_pack, "wsh", axis=0, tiled=True)
+    w_down = lax.all_gather(down_weight, "wsh", axis=0, tiled=True)
+    w_out = middle_all[:, :D]
+    w_gate_up = middle_all[:, D:]
     gain_first = gain_first.astype(jnp.float32)
     gain_second = gain_second.astype(jnp.float32)
     tokens = inputs.shape[0]
@@ -94,9 +98,10 @@
     full_length = cycle_size * tokens
     residual = inputs.reshape(rows, D).astype(jnp.float32)
     normed = rms_norm(residual, gain_first).astype(jnp.bfloat16)
-    query_pre = jnp.dot(normed, w_query, preferred_element_type=jnp.float32)
-    key_pre = jnp.dot(normed, w_key, preferred_element_type=jnp.float32)
-    value_pre = jnp.dot(normed, w_value, preferred_element_type=jnp.float32)
+    first_pre = jnp.dot(normed, w_first, preferred_element_type=jnp.float32)
+    query_pre = first_pre[:, :D]
+    key_pre = first_pre[:, D : D + pair_width]
+    value_pre = first_pre[:, D + pair_width :]
     queries = (
         rotate(query_pre.reshape(tokens, batch * HEADS, HEAD), cosine, sine)
         .astype(jnp.bfloat16)
@@ -139,20 +144,22 @@
         )
         return (weighted, total + jnp.sum(powers, axis=-1))
 
+    all_pairs = lax.all_gather(pairs, "ctx", axis=0, tiled=True)
     start_state = (
         jnp.zeros((tokens, batch, KV_HEADS, per_group, HEAD), jnp.float32),
         jnp.zeros((batch, KV_HEADS, per_group, tokens), jnp.float32),
     )
     weighted, total = sweep(
-        start_state, lax.all_gather(pairs, "ctx", axis=0, tiled=True), last_query, forward_step
+        start_state, all_pairs, last_query, forward_step
     )
     totals_moved = jnp.transpose(total, (3, 0, 1, 2))[..., None]
     mixed = weighted / totals_moved
     mixed_low = mixed.astype(jnp.bfloat16).reshape(rows, D)
     middle = residual + jnp.dot(mixed_low, w_out, preferred_element_type=jnp.float32)
     normed_two = rms_norm(middle, gain_second).astype(jnp.bfloat16)
-    gate = jnp.dot(normed_two, w_gate, preferred_element_type=jnp.float32)
-    up = jnp.dot(normed_two, w_up, preferred_element_type=jnp.float32)
+    gate_up = jnp.dot(normed_two, w_gate_up, preferred_element_type=jnp.float32)
+    gate = gate_up[:, :width]
+    up = gate_up[:, width:]
     hidden = (jax.nn.silu(gate) * up).astype(jnp.bfloat16)
     result = middle + jnp.dot(hidden, w_down, preferred_element_type=jnp.float32)
     layer_out = result.astype(jnp.bfloat16).reshape(tokens, batch, D)
@@ -161,13 +168,11 @@
     grad_hidden = jnp.einsum("nd,fd->nf", seed, w_down, preferred_element_type=jnp.float32)
     unused_value, swiglu_back = jax.vjp(lambda left, right: jax.nn.silu(left) * right, gate, up)
     grad_gate_f, grad_up_f = swiglu_back(grad_hidden)
-    gate_back = grad_gate_f.astype(jnp.bfloat16)
-    up_back = grad_up_f.astype(jnp.bfloat16)
-    grad_wgate = jnp.einsum("nd,nf->df", normed_two, gate_back, preferred_element_type=jnp.float32)
-    grad_wup = jnp.einsum("nd,nf->df", normed_two, up_back, preferred_element_type=jnp.float32)
-    grad_normed_two = jnp.einsum(
-        "nf,df->nd", gate_back, w_gate, preferred_element_type=jnp.float32
-    ) + jnp.einsum("nf,df->nd", up_back, w_up, preferred_element_type=jnp.float32)
+    back = jnp.concatenate(
+        [grad_gate_f.astype(jnp.bfloat16), grad_up_f.astype(jnp.bfloat16)], axis=1
+    )
+    grad_gate_up = jnp.einsum("nd,nf->df", normed_two, back, preferred_element_type=jnp.float32)
+    grad_normed_two = jnp.einsum("nf,df->nd", back, w_gate_up, preferred_element_type=jnp.float32)
     unused_norm, second_norm_back = jax.vjp(rms_norm, middle, gain_second)
     grad_middle_norm, grad_gain_second = second_norm_back(grad_normed_two)
     grad_middle = seed.astype(jnp.float32) + grad_middle_norm
@@ -178,6 +183,13 @@
     ).reshape(tokens, batch, KV_HEADS, per_group, HEAD)
     scaled = (grad_mixed / totals_moved).astype(jnp.bfloat16)
     offset = jnp.sum(grad_mixed * mixed, axis=-1) / totals_moved[..., 0]
+    middle_grads = jnp.concatenate([grad_project, grad_gate_up], axis=1).astype(jnp.bfloat16)
+    down_grads = grad_down.astype(jnp.bfloat16)
+    middle_grads, down_grads, scaled, offset = lax.optimization_barrier(
+        (middle_grads, down_grads, scaled, offset)
+    )
+    down_share = lax.psum_scatter(down_grads, "wsh", scatter_dimension=0, tiled=True)
+    middle_share = lax.psum_scatter(middle_grads, "wsh", scatter_dimension=0, tiled=True)
     offset_moved = jnp.transpose(offset, (1, 2, 3, 0))[..., None]
 
     def backward_step(state, piece, first):
@@ -222,9 +234,11 @@
         jnp.zeros((full_length, batch, 2 * pair_width), jnp.float32),
     )
     grad_queries, grad_pairs = sweep(
-        back_state, lax.all_gather(pairs, "ctx", axis=0, tiled=True), last_query, backward_step
-    )
-    own_pairs = lax.psum_scatter(grad_pairs, "ctx", scatter_dimension=0, tiled=True)
+        back_state, all_pairs, last_query, backward_step
+    )
+    own_pairs = lax.psum_scatter(
+        grad_pairs.astype(jnp.bfloat16), "ctx", scatter_dimension=0, tiled=True
+    ).astype(jnp.float32)
     query_back = (
         rotate(grad_queries.reshape(tokens, batch * HEADS, HEAD), cosine, -sine)
         .astype(jnp.bfloat16)
@@ -236,56 +250,31 @@
         .reshape(rows, pair_width)
     )
     value_back = own_pairs[..., pair_width:].astype(jnp.bfloat16).reshape(rows, pair_width)
-    grad_wquery = jnp.einsum("nd,nk->dk", normed, query_back, preferred_element_type=jnp.float32)
-    grad_wkey = jnp.einsum("nd,nk->dk", normed, key_back, preferred_element_type=jnp.float32)
-    grad_wvalue = jnp.einsum("nd,nk->dk", normed, value_back, preferred_element_type=jnp.float32)
-    grad_normed = jnp.einsum("nk,dk->nd", query_back, w_query, preferred_element_type=jnp.float32)
-    grad_normed = grad_normed + jnp.einsum(
-        "nk,dk->nd", key_back, w_key, preferred_element_type=jnp.float32
-    )
-    grad_normed = grad_normed + jnp.einsum(
-        "nk,dk->nd", value_back, w_value, preferred_element_type=jnp.float32
-    )
+    first_back = jnp.concatenate([query_back, key_back, value_back], axis=1)
+    grad_first = jnp.einsum("nd,nk->dk", normed, first_back, preferred_element_type=jnp.float32)
+    grad_normed = jnp.einsum("nk,dk->nd", first_back, w_first, preferred_element_type=jnp.float32)
     unused_first, first_norm_back = jax.vjp(rms_norm, residual, gain_first)
     grad_residual, grad_gain_first = first_norm_back(grad_normed)
     input_grad = (grad_middle + grad_residual).astype(jnp.bfloat16).reshape(tokens, batch, D)
-    shares = (
-        lax.psum_scatter(grad_wquery, "wsh", scatter_dimension=0, tiled=True),
-        lax.psum_scatter(grad_wkey, "wsh", scatter_dimension=0, tiled=True),
-        lax.psum_scatter(grad_wvalue, "wsh", scatter_dimension=0, tiled=True),
-        lax.psum_scatter(grad_project, "wsh", scatter_dimension=0, tiled=True),
-        lax.psum_scatter(grad_wgate, "wsh", scatter_dimension=0, tiled=True),
-        lax.psum_scatter(grad_wup, "wsh", scatter_dimension=0, tiled=True),
-        lax.psum_scatter(grad_down, "wsh", scatter_dimension=0, tiled=True),
-        lax.psum_scatter(grad_gain_first, "wsh", scatter_dimension=0, tiled=True),
-        lax.psum_scatter(grad_gain_second, "wsh", scatter_dimension=0, tiled=True),
-    )
-    owned = lax.psum(
-        (
-            shares[0],
-            shares[1],
-            shares[2],
-            shares[3],
-            shares[4],
-            shares[5],
-            shares[6],
-            shares[7],
-            shares[8],
-        ),
-        "ctx",
-    )
+    first_grads = jnp.concatenate(
+        [grad_first, grad_gain_first[:, None], grad_gain_second[:, None]], axis=1
+    ).astype(jnp.bfloat16)
+    first_share = lax.psum_scatter(first_grads, "wsh", scatter_dimension=0, tiled=True)
+    down_own = lax.psum(down_share, "ctx").astype(jnp.float32)
+    middle_own = lax.psum(middle_share, "ctx").astype(jnp.float32)
+    first_own = lax.psum(first_share, "ctx").astype(jnp.float32)
     return (
         layer_out,
         input_grad,
-        owned[0],
-        owned[1],
-        owned[2],
-        owned[3],
-        owned[4],
-        owned[5],
-        owned[6],
-        owned[7],
-        owned[8],
+        first_own[:, :D],
+        first_own[:, D : D + pair_width],
+        first_own[:, D + pair_width : D + 2 * pair_width],
+        middle_own[:, :D],
+        middle_own[:, D : D + width],
+        middle_own[:, D + width :],
+        down_own,
+        first_own[:, D + 2 * pair_width],
+        first_own[:, D + 2 * pair_width + 1],
     )
 
 

time: 810 us -> 594 us (0.73)
  waiting for transfers between devices: 512 us -> 364 us
  blocking collectives: 68.2 us -> 0 us
    reduce_scatter x8 -> x3, waiting for transfers between devices: 346 us -> 172 us  [the longest x1 97.6 us: local(): lax.psum_scatter(grad_pairs.astype(jnp.bfloat16), 'ctx', scatter_dimensio...]
    all_gather x4 -> x0, blocking collectives: 29.8 us -> none  [the longest x1 9.41 us: local(): lax.all_gather(output_weight, 'wsh', axis=0, tiled=True)]
    psum x1 -> x0, blocking collectives: 23.3 us -> none  [local(): lax.psum((shares[0], shares[1], shares[2], shares[3], shares[4], shares[5...]
    all_gather x4, waiting for transfers between devices: 61.5 us -> 82.7 us  [the longest x1 45.2 us: local(): all_pairs = lax.all_gather(pairs, 'ctx', axis=0, tiled=True)]
    unnamed x13 -> x10, waiting for transfers between devices: 2.06 us -> 22.7 us
    unnamed x2 -> x0, blocking collectives: 15.2 us -> none
    psum x1, waiting for transfers between devices: 102 us -> 86.9 us  [local(): middle_own = lax.psum(middle_share, 'ctx').astype(jnp.float32)]
    unnamed x151 -> x91, local copies, waits for them, and re-layouts: 36.2 us -> 23.5 us
  transfers between devices with their start and end apart: 13 -> 9, of which waited for: 12 -> 9; matrix products, arithmetic and copies ran while one was open for 13% -> 16% of each run, Pallas kernels for 0% -> 0%
where the time goes in v1:
time: 594 us; the launch traced here: 585 us
  waiting for transfers between devices  364 us (61%)
  local copies, waits for them, and re-layouts  89.1 us (15%)
  matrix products  82.9 us (14%)
  other arithmetic  33.6 us (6%)
  between operations  15 us (3%)
    reduce_scatter x1, waiting for transfers between devices, local(): lax.psum_scatter(grad_pairs.astype(jnp.bfloat16), 'ctx', scatter_dimensio...  97.6 us
    psum x1, waiting for transfers between devices, local(): middle_own = lax.psum(middle_share, 'ctx').astype(jnp.float32)  86.9 us
    reduce_scatter x1, waiting for transfers between devices, local(): lax.psum_scatter(middle_grads, 'wsh', scatter_dimension=0, tiled=True)  45.8 us
    all_gather x1, waiting for transfers between devices, local(): all_pairs = lax.all_gather(pairs, 'ctx', axis=0, tiled=True)  45.2 us
    reduce_scatter x1, waiting for transfers between devices, local(): lax.psum_scatter(first_grads, 'wsh', scatter_dimension=0, tiled=True)  28.3 us
    unnamed x91, local copies, waits for them, and re-layouts  23.5 us
    unnamed x10, waiting for transfers between devices  22.7 us
    all_gather x1, waiting for transfers between devices, local(): middle_all = lax.all_gather(middle_pack, 'wsh', axis=0, tiled=True)  13.4 us
  transfers between devices with their start and end apart: 9, of which 9 were waited for; matrix products, arithmetic and copies ran while one was open for 16% of the time, Pallas kernels for 0%

profile of v1, /device:TPU:0, one launch (start us, length us, event | category | flops | bytes accessed | tf_op | source)
XLA Modules:
  0.0 585.5 jit_solution(14721523115991597420)
XLA Ops:
  18.5 12.4 %all-gather.5.cloned.1.call-done = bf16[576,962]{1,0:T(8,128)(2,1)} async-done(((bf16[144,962]{1,0:T(8,128)(2,1)}), bf16[576,962]{1,0:T(8,128)(2,1)}) %all-gather.5.cloned.1.call-update) | async-done | bytes 1108240 | tf_op jit(solution)/shard_map/all_gather | solution.py:71
  44.6 3.3 concatenate.53
  62.5 45.2 %all-gather.7.cloned.1.call-done = bf16[2048,2,384]{0,2,1:T(8,128)(2,1)} async-done(((bf16[256,2,384]{0,2,1:T(8,128)(2,1)}), bf16[2048,2,384]{0,2,1:T(8,128)(2,1)}) %all-gather.7.cloned.1.call-update) | async-done | bytes 3145744 | tf_op jit(solution)/shard_map/all_gather | solution.py:147
  107.9 10.0 %while.26 = (s32[]{:T(128)}, f32[256,2,3,3,64]{0,4,3,2,1:T(8,128)S(1)}, f32[2,3,3,256]{3,2,1,0:T(4,128)S(1)}, s32[]{:T(128)}, bf16[2048,2,384]{0,2,1:T(8,128)(2,...) while((s32[]{:T(128)}, ...), condition=%wide.region_3.4_spmd.clone, body=%wide.region_1.3_spmd.clone.sunk | while | flops 1236829440 | bytes 46287048 | solution.py:52
  110.1 4.3 fusion.105
  114.4 3.4 fusion.106
  117.9 2.9 copy.167
  121.3 4.8 fusion.54
  126.2 2.9 reshape.251
  129.1 13.4 %all-gather.9.cloned.1.call-done = bf16[576,3648]{1,0:T(8,128)(2,1)} async-done(((bf16[144,3648]{1,0:T(8,128)(2,1)}), bf16[576,3648]{1,0:T(8,128)(2,1)}) %all-gather.9.cloned.1.call-update) | async-done | bytes 4202512 | tf_op jit(solution)/shard_map/all_gather | solution.py:80
  145.3 7.7 %fusion.33 = f32[512,3072]{1,0:T(8,128)} fusion(bf16[576,3648]{1,0:T(8,128)(2,1)} %all-gather.9.cloned.1.call-done, f32[512,576]{0,1:T(8,128)S(1)} %get-tuple-element.329, f32[576]{0:T(1024)S(1)} %get-tuple-element.257, f32[512]{0:T(512)S(1)} %fusion.49), kind=kOutput, calls=%fused_computation.55 | convolution fusion | flops 1812824064 | bytes 11014400 | tf_op jit(solution)/shard_map/dot_general | solution.py:160
  153.0 11.6 %all-gather.11.cloned.1.call-done = bf16[1536,576]{0,1:T(8,128)(2,1)} async-done(((bf16[384,576]{0,1:T(8,128)(2,1)}), bf16[1536,576]{0,1:T(8,128)(2,1)}) %all-gather.11.cloned.1.call-update) | async-done | bytes 1769488 | tf_op jit(solution)/shard_map/all_gather | solution.py:81
  164.7 5.9 %fusion.29 = (bf16[512,1536]{1,0:T(8,128)(2,1)S(1)}, bf16[512,1536]{1,0:T(8,128)(2,1)S(1)}, bf16[512,1536]{1,0:T(8,128)(2,1)S(1)}) fusion(f32[512,3072]{1,0:T(8,128)} %fusion.33, bf16[512,576]{1,0:T(8,128)(2,1)} %copy-done.20, bf16[1536,576]{0,1:T(8,128)(2,1)} %all-gather.11.cloned.1.call-done), kind=kOutput, calls=%fused_computation.41 | convolution fusion | flops 918552576 | bytes 13369344 | tf_op jit(solution)/shard_map/nd,fd->nf/dot_general | solution.py:168
  170.6 3.8 convolution_convert_fusion
  174.4 4.9 multiply_reduce_fusion.1
  183.7 3.0 fusion.43
  186.8 4.3 reshape.254
  191.0 6.6 %multiply_reduce_fusion = (f32[256,2,3,3]{3,2,1,0:T(4,128)S(1)}, bf16[256,2,3,3,64]{4,3,2,1,0:T(4,128)(2,1)}) fusion(f32[256,2,3,3,64]{4,3,2,1,0:T(4,128)} %reshape.254, f32[256,2,3,3,64]{4,3,2,1,0:T(4,128)} %copy.167, f32[256,2,3,3]{3,2,1,0:T(4,128)S(1)} %bitcast.162), kind=kLoop, calls=%fused_computation.45 | loop fusion | flops 1469952 | bytes 2985984 | tf_op jit(solution)/shard_map/reduce_sum | solution.py:185
  198.9 4.0 pad_maximum_fusion
  207.7 39.0 %while.27 = (s32[]{:T(128)}, f32[256,2,3,3,64]{0,4,3,2,1:T(8,128)S(1)}, bf16[2048,2,384]{0,2,1:T(8,128)(2,1)}, s32[]{:T(128)}, bf16[2048,2,384]{0,2,1:T(8,128)(2...) while((s32[]{:T(128)}, ...), condition=%wide.region_8.9_spmd.clone, body=%wide.region_7.8_spmd.clone.sunk | while | flops 3062433024 | bytes 163606848 | solution.py:52
  209.2 7.9 %fusion.117 = f32[2,3,1024,256,3]{3,2,4,1,0:T(8,128)} fusion(bf16[1024,2,3,64,1]{0,3,4,2,1:T(8,128)(2,1)S(1)} %bitcast.153, bf16[256,2,3,3,64]{0,4,3,2,1:T(8,128)(2,1)S(1)} %get-tuple-element.513), kind=kOutput, calls=%fused_computation.123.clone.1 | convolution fusion | flops 603979776 | bytes 20250624 | tf_op jit(solution)/shard_map/while/body/qsgrd,ksgd->sgrqk/dot_general | solution.py:128
  217.3 8.9 %fusion.118 = bf16[2,3,3,256,1024]{3,4,2,1,0:T(8,128)(2,1)S(1)} fusion(f32[2,3,1024,256,3]{3,2,4,1,0:T(8,128)} %fusion.117, f32[2,3,3,256]{3,2,1,0:T(4,128)S(1)} %bitcast.168, pred[256,1024]{0,1:T(8,128)(4,1)S(1)} %broadcast_compare_fusion.5, bf16[1024,2,3,64,1]{0,3,4,2,1:T(8,128)(2,1)S(1)} %bitcast.159, ...), kind=kOutput, calls=%fused_computation.18.clone.1 | convolution fusion | flops 627572736 | bytes 29968384 | tf_op jit(solution)/shard_map/while/body/qsgrd,ksgd->sgrqk/dot_general | solution.py:199
  229.9 8.1 %fusion.120 = bf16[2,3,1024,64,1]{2,3,4,1,0:T(8,128)(2,1)S(1)} fusion(bf16[256,2,3,3,64]{0,4,3,2,1:T(8,128)(2,1)S(1)} %get-tuple-element.514, f32[2,3,1024,256,3]{3,2,4,1,0:T(8,128)} %fusion.117, pred[256,1024]{0,1:T(8,128)(4,1)S(1)} %broadcast_compare_fusion.5), kind=kOutput, calls=%fused_computation.21.clone.1 | convolution fusion | flops 618135552 | bytes 20512768 | tf_op jit(solution)/shard_map/while/body/sgrqk,qsgrd->ksgd/dot_general | solution.py:216
  238.0 6.8 %bitcast_multiply_fusion.2 = bf16[2,3,1024,64]{2,3,1,0:T(8,128)(2,1)S(1)} fusion(bf16[2,3,3,256,1024]{3,4,2,1,0:T(8,128)(2,1)} %copy-done, bf16[256,2,3,3,64]{0,4,3,2,1:T(8,128)(2,1)S(1)} %get-tuple-element.513), kind=kOutput, calls=%fused_computation.24.clone.1 | convolution fusion | flops 604766208 | bytes 10813440 | tf_op jit(solution)/shard_map/while/body/sgrqk,qsgrd->ksgd/dot_general | solution.py:211
  254.6 3.1 copy.202
  263.3 97.6 %reduce-scatter.7.cloned.1.call-done = bf16[256,2,384]{0,2,1:T(8,128)(2,1)} async-done(((bf16[2048,2,384]{0,2,1:T(8,128)(2,1)}), bf16[256,2,384]{0,2,1:T(8,128)(2,1)}) %reduce-scatter.7.cloned.1.call-update) | async-done | bytes 393232 | tf_op jit(solution)/shard_map/reduce_scatter | solution.py:239
  365.6 3.5 multiply_reduce_fusion.2
  371.3 21.9 %reduce-scatter.13.cloned.1.call-done = bf16[384,576]{1,0:T(8,128)(2,1)} async-done(((bf16[1536,576]{1,0:T(8,128)(2,1)}), bf16[384,576]{1,0:T(8,128)(2,1)}) %reduce-scatter.13.cloned.1.call-update) | async-done | bytes 442384
  395.2 45.8 %reduce-scatter.11.cloned.1.call-done = bf16[144,3648]{1,0:T(8,128)(2,1)} async-done(((bf16[576,3648]{1,0:T(8,128)(2,1)}), bf16[144,3648]{1,0:T(8,128)(2,1)}) %reduce-scatter.11.cloned.1.call-update) | async-done | bytes 1050640 | tf_op jit(solution)/shard_map/reduce_scatter | solution.py:192
  441.0 28.3 %reduce-scatter.9.cloned.1.call-done = bf16[144,962]{1,0:T(8,128)(2,1)} async-done(((bf16[576,962]{1,0:T(8,128)(2,1)}), bf16[144,962]{1,0:T(8,128)(2,1)}) %reduce-scatter.9.cloned.1.call-update) | async-done | bytes 277072 | tf_op jit(solution)/shard_map/reduce_scatter | solution.py:262
  469.3 3.9 fusion.35
  483.1 86.9 %all-reduce.3.cloned.1.call-done = (bf16[144,3648]{1,0:T(8,128)(2,1)}, bf16[144,962]{1,0:T(8,128)(2,1)}, bf16[384,576]{0,1:T(8,128)(2,1)}) async-done(((bf16[144,3648]{1,0:T(8,128)(2,1)}, bf16[144,962]{1,0:T(8,128)(2,1)}, bf16[384,576]{0,1:T(8,128)(2,1)}), (bf16[144,3648]{1,0:T(8,128)(2,1)}, bf16[144,962]{1,0:T(8,128)(2,1)}, bf16[384,576]{0,1:T(8,128)(2,1)})) %all-reduce.3.cloned.1.call-update) | async-done | bytes 1770064 | tf_op jit(solution)/shard_map/psum | solution.py:264
  (202 shorter events, 102.6 us)
Async XLA Ops:
  7.2 23.7 %all-gather.5.cloned.1.call-start = ((), (), s32[]{:S(2)}) async-start(), calls=%async_computation.4 | async-start | bytes 1474560 | tf_op jit(solution)/shard_map/all_gather | solution.py:71
  10.6 97.1 %all-gather.7.cloned.1.call-start = ((), (), s32[]{:S(2)}) async-start(), calls=%async_computation.5 | async-start | bytes 3538944 | tf_op jit(solution)/shard_map/all_gather | solution.py:147
  16.1 18.4 %copy-start.1 = (f32[512,576]{0,1:T(8,128)}, f32[512,576]{0,1:T(8,128)S(1)}, u32[]{:S(2)}) copy-start(f32[512,576]{0,1:T(8,128)S(1)} %copy.168) | copy-start | bytes 3538948
  17.2 14.9 %copy-start.39 = (f32[512]{0:T(512)}, f32[512]{0:T(512)S(1)}, u32[]{:S(2)}) copy-start(f32[512]{0:T(512)S(1)} %add.132) | copy-start | bytes 6148
  17.3 17.3 %copy-start.36 = (f32[512]{0:T(512)}, f32[512]{0:T(512)S(1)}, u32[]{:S(2)}) copy-start(f32[512]{0:T(512)S(1)} %rsqrt.22) | copy-start | bytes 6148
  18.5 38.4 %copy-start.16 = (f32[256,32]{1,0:T(8,128)}, f32[256,32]{1,0:T(8,128)S(1)}, u32[]{:S(2)}) copy-start(f32[256,32]{1,0:T(8,128)S(1)} %get-tuple-element.327) | copy-start | bytes 98308
  41.1 3.5 copy-start.31
  44.5 3.5 copy-start.28
  44.5 98.0 %all-gather.9.cloned.1.call-start = ((), (), s32[]{:S(2)}) async-start(), calls=%async_computation.6 | async-start | bytes 5345280 | tf_op jit(solution)/shard_map/all_gather | solution.py:80
  47.9 116.7 %all-gather.11.cloned.1.call-start = ((), (), s32[]{:S(2)}) async-start(), calls=%async_computation.7 | async-start | bytes 2211840 | tf_op jit(solution)/shard_map/all_gather | solution.py:81
  62.4 298.5 %reduce-scatter.7.cloned.1.call-start = ((), (), s32[]{:S(2)}) async-start(), calls=%async_computation.8 | async-start | bytes 3538944 | tf_op jit(solution)/shard_map/reduce_scatter | solution.py:239
  126.2 16.3 %copy-start.2 = (f32[512,576]{0,1:T(8,128)S(1)}, f32[512,576]{0,1:T(8,128)}, u32[]{:S(2)}) copy-start(f32[512,576]{0,1:T(8,128)} %copy-done.1) | copy-start | bytes 3538948
  153.0 17.6 %copy-start.9 = (f32[512,576]{0,1:T(8,128)S(1)}, f32[512,576]{0,1:T(8,128)}, u32[]{:S(2)}) copy-start(f32[512,576]{0,1:T(8,128)} %copy-done.8) | copy-start | bytes 3538948
  170.6 10.8 %copy-start.42 = (bf16[512,1536]{1,0:T(8,128)(2,1)}, bf16[512,1536]{1,0:T(8,128)(2,1)S(1)}, u32[]{:S(2)}) copy-start(bf16[512,1536]{1,0:T(8,128)(2,1)S(1)} %get-tuple-element.306) | copy-start | bytes 4718596
  174.4 4.9 copy-start.23
  179.7 4.0 copy-start.4
  191.0 7.9 %copy-start.15 = (bf16[576,3072]{1,0:T(8,128)(2,1)S(1)}, bf16[576,3072]{1,0:T(8,128)(2,1)}, u32[]{:S(2)}) copy-start(bf16[576,3072]{1,0:T(8,128)(2,1)} %convolution_convert_fusion) | copy-start | bytes 10616836
  198.9 4.0 copy-start.11
  226.2 3.6 copy-start
  238.0 6.8 %copy-start.6 = (bf16[2048,2,384]{0,2,1:T(8,128)(2,1)S(1)}, bf16[2048,2,384]{0,2,1:T(8,128)(2,1)}, u32[]{:S(2)}) copy-start(bf16[2048,2,384]{0,2,1:T(8,128)(2,1)} %get-tuple-element.496) | copy-start | bytes 9437188 | tf_op jit(solution)/shard_map/while
  246.6 146.6 %reduce-scatter.13.cloned.1.call-start = ((), (), s32[]{:S(2)}) async-start(), calls=%async_computation.11 | async-start | bytes 2457600
  250.6 190.4 %reduce-scatter.11.cloned.1.call-start = ((), (), s32[]{:S(2)}) async-start(), calls=%async_computation.10 | async-start | bytes 5345280 | tf_op jit(solution)/shard_map/reduce_scatter | solution.py:192
  251.3 217.9 %reduce-scatter.9.cloned.1.call-start = ((), (), s32[]{:S(2)}) async-start(), calls=%async_computation.9 | async-start | bytes 1474560 | tf_op jit(solution)/shard_map/reduce_scatter | solution.py:262
  254.6 3.2 copy-start.17
  365.6 3.6 copy-start.27
  371.3 98.1 %copy-start.10 = (f32[512,576]{0,1:T(8,128)S(1)}, f32[512,576]{0,1:T(8,128)}, u32[]{:S(2)}) copy-start(f32[512,576]{0,1:T(8,128)} %copy-done.8) | copy-start | bytes 3538948
  371.3 198.6 %all-reduce.3.cloned.1.call-start = ((), (), s32[]{:S(2)}) async-start(), calls=%async_computation.12 | async-start | bytes 3612672 | tf_op jit(solution)/shard_map/psum | solution.py:264
  473.2 5.5 copy-start.40
  473.2 5.5 copy-start.5
  473.2 5.5 copy-start.35
  473.2 5.5 copy-start.38
  569.9 5.2 copy-start.13
  (20 other events, 33.6 us)
Sparse Core Ops, SparseCore 0:
  10.7 20.1 all-gather.4
  44.6 63.0 all-gather.6
  109.3 33.1 all-gather.8
  143.9 20.7 all-gather.10
  246.7 114.1 reduce-scatter.6
  363.3 29.8 reduce-scatter.12
  395.9 45.0 reduce-scatter.10
  443.6 25.6 reduce-scatter.8
  474.3 95.6 all-reduce.2

commit v2 on v1

--- a/solution.py
+++ b/solution.py
@@ -1,8 +1,11 @@
+import functools
 import math
 
 import jax
 import jax.numpy as jnp
 from jax import lax
+from jax.experimental import pallas as pl
+from jax.experimental.pallas import tpu as pltpu
 from jax.sharding import PartitionSpec as P
 
 D = 576
@@ -50,6 +53,159 @@
         return step(carry, piece, begin)
 
     return lax.fori_loop(0, upper, advance, state)
+
+
+COPIES = 10
+
+
+def part_of(ref, rows, cols, by_cols, begin, count, pieces):
+    if by_cols:
+        size = cols // pieces
+        return ref.at[:, pl.ds(pl.multiple_of(begin * size, 128), count * size)]
+    size = rows // pieces
+    return ref.at[pl.ds(pl.multiple_of(begin * size, 16), count * size), :]
+
+
+def add_into(out_ref, terms, rows):
+    @pl.loop(0, rows // 16)
+    def _(index):
+        at = pl.ds(pl.multiple_of(index * 16, 16), 16)
+        total = terms[0][at, :].astype(jnp.float32)
+        for term in terms[1:]:
+            total = total + term[at, :].astype(jnp.float32)
+        out_ref[at, :] = total.astype(out_ref.dtype)
+
+
+def reduce_kernel(shapes, *refs):
+    n = len(shapes)
+    ins, outs = refs[:n], refs[n : 2 * n]
+    scratch = refs[2 * n : 2 * n + 8 * n]
+    send_sem, recv_sem = refs[2 * n + 8 * n :]
+    wsh = lax.axis_index("wsh")
+    ctx = lax.axis_index("ctx")
+    high, low = wsh // 2, wsh % 2
+    far, near = ctx // 2, ctx % 2
+    pair_low = {"ctx": ctx, "wsh": high * 2 + (1 - low)}
+    pair_high = {"ctx": ctx, "wsh": (1 - high) * 2 + low}
+    pair_near = {"ctx": far * 2 + (1 - near), "wsh": wsh}
+    others = [(far + 1 + k) % 4 for k in range(3)]
+    pair_far = [{"ctx": other * 2 + near, "wsh": wsh} for other in others]
+
+    barrier = pltpu.get_barrier_semaphore()
+    for device in [pair_low, pair_high, pair_near] + pair_far:
+        pl.semaphore_signal(barrier, inc=1, device_id=device, device_id_type=pl.DeviceIdType.MESH)
+    pl.semaphore_wait(barrier, 6)
+
+    started = {}
+
+    def send(chunk, index, source, target, device):
+        copy = pltpu.make_async_remote_copy(
+            src_ref=source,
+            dst_ref=target,
+            send_sem=send_sem.at[chunk, index],
+            recv_sem=recv_sem.at[chunk, index],
+            device_id=device,
+            device_id_type=pl.DeviceIdType.MESH,
+        )
+        copy.start()
+        started[chunk, index] = copy
+
+    def step(stage, chunk):
+        rows, cols, by_cols = shapes[chunk]
+        term, out = ins[chunk], outs[chunk]
+        got_low, sum_low, got_high, sum_high, got_near, sum_near, got_far, full = scratch[
+            8 * chunk : 8 * chunk + 8
+        ]
+        half_rows = rows if by_cols else rows // 2
+        half_cols = cols // 2 if by_cols else cols
+        piece_rows = rows if by_cols else rows // 8
+
+        def half(ref, which):
+            return part_of(ref, rows, cols, by_cols, which * 4, 4, 8)
+
+        def piece(ref, which):
+            return part_of(ref, rows, cols, by_cols, near * 4 + which, 1, 8)
+
+        def quarter(ref, which):
+            return part_of(ref, half_rows, half_cols, by_cols, which, 1, 4)
+
+        if stage == 0:
+            send(chunk, 0, term.at[:, 1 - low], got_low, pair_low)
+        elif stage == 1:
+            started[chunk, 0].wait_recv()
+            for index in range(2):
+                add_into(sum_low.at[index], [term.at[index, low], got_low.at[index]], rows)
+            send(chunk, 1, sum_low.at[1 - high], got_high, pair_high)
+        elif stage == 2:
+            started[chunk, 1].wait_recv()
+            add_into(sum_high, [sum_low.at[high], got_high], rows)
+            send(chunk, 2, half(sum_high, 1 - near), got_near, pair_near)
+        elif stage == 3:
+            started[chunk, 2].wait_recv()
+            add_into(sum_near, [half(sum_high, near), got_near], half_rows)
+            for k in range(3):
+                send(chunk, 3 + k, quarter(sum_near, others[k]), got_far.at[k], pair_far[k])
+        elif stage == 4:
+            for k in range(3):
+                started[chunk, 3 + k].wait_recv()
+            add_into(
+                piece(full, far),
+                [quarter(sum_near, far)] + [got_far.at[k] for k in range(3)],
+                piece_rows,
+            )
+            for k in range(3):
+                send(chunk, 6 + k, piece(full, far), piece(full, far), pair_far[k])
+        elif stage == 5:
+            for k in range(3):
+                started[chunk, 6 + k].wait_recv()
+            send(chunk, 9, half(full, near), half(full, near), pair_near)
+        else:
+            started[chunk, 9].wait_recv()
+            add_into(out, [full], rows)
+
+    for turn in range(n + 6):
+        for stage in range(6, -1, -1):
+            chunk = turn - stage
+            if 0 <= chunk < n:
+                step(stage, chunk)
+    for copy in started.values():
+        copy.wait_send()
+
+
+def reduce_all(terms, by_cols, collective_id):
+    shapes = tuple((term.shape[1], term.shape[2], cut) for term, cut in zip(terms, by_cols))
+    scratch = []
+    size = 0
+    for rows, cols, cut in shapes:
+        half_shape = (rows, cols // 2) if cut else (rows // 2, cols)
+        piece_shape = (rows, cols // 8) if cut else (rows // 8, cols)
+        for shape in (
+            (2, rows, cols),
+            (2, rows, cols),
+            (rows, cols),
+            (rows, cols),
+            half_shape,
+            half_shape,
+            (3,) + piece_shape,
+            (rows, cols),
+        ):
+            scratch.append(pltpu.VMEM(shape, jnp.bfloat16))
+        size += rows * cols * 2
+    count = len(shapes)
+    return pl.pallas_call(
+        functools.partial(reduce_kernel, shapes),
+        out_shape=[jax.ShapeDtypeStruct((rows, cols), jnp.float32) for rows, cols, _ in shapes],
+        in_specs=[pl.BlockSpec(memory_space=pltpu.VMEM)] * count,
+        out_specs=[pl.BlockSpec(memory_space=pltpu.VMEM)] * count,
+        scratch_shapes=scratch
+        + [pltpu.SemaphoreType.DMA((count, COPIES)), pltpu.SemaphoreType.DMA((count, COPIES))],
+        compiler_params=pltpu.CompilerParams(
+            collective_id=collective_id, has_side_effects=True, vmem_limit_bytes=48 * 1024 * 1024
+        ),
+        cost_estimate=pl.CostEstimate(
+            flops=size * 8, bytes_accessed=size * 100, transcendentals=0
+        ),
+    )(*[term.reshape(2, 2, *term.shape[1:]) for term in terms])
 
 
 def local(
@@ -183,13 +339,23 @@
     ).reshape(tokens, batch, KV_HEADS, per_group, HEAD)
     scaled = (grad_mixed / totals_moved).astype(jnp.bfloat16)
     offset = jnp.sum(grad_mixed * mixed, axis=-1) / totals_moved[..., 0]
-    middle_grads = jnp.concatenate([grad_project, grad_gate_up], axis=1).astype(jnp.bfloat16)
-    down_grads = grad_down.astype(jnp.bfloat16)
-    middle_grads, down_grads, scaled, offset = lax.optimization_barrier(
-        (middle_grads, down_grads, scaled, offset)
-    )
-    down_share = lax.psum_scatter(down_grads, "wsh", scatter_dimension=0, tiled=True)
-    middle_share = lax.psum_scatter(middle_grads, "wsh", scatter_dimension=0, tiled=True)
+    direct = cycle_size == 8 and lax.axis_size("wsh") == 4
+    owners = lax.axis_size("wsh")
+    if direct:
+        spare = -(D + 2 * width) % 1024
+        middle_grads = jnp.concatenate(
+            [grad_gate_up, grad_project, jnp.zeros((D, spare), jnp.float32)], axis=1
+        ).astype(jnp.bfloat16)
+        middle_terms = [
+            middle_grads[:, at : at + 1024].reshape(owners, D // owners, 1024)
+            for at in range(0, middle_grads.shape[1], 1024)
+        ]
+        down_term = grad_down.astype(jnp.bfloat16).reshape(owners, width // owners, D)
+    else:
+        middle_grads = jnp.concatenate([grad_gate_up, grad_project], axis=1).astype(jnp.bfloat16)
+        down_grads = grad_down.astype(jnp.bfloat16)
+        middle_share = lax.psum_scatter(middle_grads, "wsh", scatter_dimension=0, tiled=True)
+        down_share = lax.psum_scatter(down_grads, "wsh", scatter_dimension=0, tiled=True)
     offset_moved = jnp.transpose(offset, (1, 2, 3, 0))[..., None]
 
     def backward_step(state, piece, first):
@@ -256,22 +422,33 @@
     unused_first, first_norm_back = jax.vjp(rms_norm, residual, gain_first)
     grad_residual, grad_gain_first = first_norm_back(grad_normed)
     input_grad = (grad_middle + grad_residual).astype(jnp.bfloat16).reshape(tokens, batch, D)
-    first_grads = jnp.concatenate(
-        [grad_first, grad_gain_first[:, None], grad_gain_second[:, None]], axis=1
-    ).astype(jnp.bfloat16)
-    first_share = lax.psum_scatter(first_grads, "wsh", scatter_dimension=0, tiled=True)
-    down_own = lax.psum(down_share, "ctx").astype(jnp.float32)
-    middle_own = lax.psum(middle_share, "ctx").astype(jnp.float32)
-    first_own = lax.psum(first_share, "ctx").astype(jnp.float32)
+    first_grads = [grad_first, grad_gain_first[:, None], grad_gain_second[:, None]]
+    if direct:
+        spare = -(D + 2 * pair_width + 2) % 1024
+        first_grads.append(jnp.zeros((D, spare), jnp.float32))
+    first_grads = jnp.concatenate(first_grads, axis=1).astype(jnp.bfloat16)
+    if direct:
+        count = len(middle_terms)
+        sums = reduce_all(middle_terms + [down_term], [True] * count + [False], 1)
+        middle_own = jnp.concatenate(sums[:count], axis=1)
+        down_own = sums[count]
+        first_own = reduce_all(
+            [first_grads.reshape(owners, D // owners, first_grads.shape[1])], [True], 2
+        )[0]
+    else:
+        first_share = lax.psum_scatter(first_grads, "wsh", scatter_dimension=0, tiled=True)
+        down_own = lax.psum(down_share, "ctx").astype(jnp.float32)
+        middle_own = lax.psum(middle_share, "ctx").astype(jnp.float32)
+        first_own = lax.psum(first_share, "ctx").astype(jnp.float32)
     return (
         layer_out,
         input_grad,
         first_own[:, :D],
         first_own[:, D : D + pair_width],
         first_own[:, D + pair_width : D + 2 * pair_width],
-        middle_own[:, :D],
-        middle_own[:, D : D + width],
-        middle_own[:, D + width :],
+        middle_own[:, 2 * width : 2 * width + D],
+        middle_own[:, :width],
+        middle_own[:, width : 2 * width],
         down_own,
         first_own[:, D + 2 * pair_width],
         first_own[:, D + 2 * pair_width + 1],

time: 594 us -> 453 us (0.76)
  waiting for transfers between devices: 364 us -> 83.6 us
  Pallas kernels: 0 us -> 149 us
    pallas_call x0 -> x2, Pallas kernels: none -> 149 us  [reduce_all(): pl.pallas_call(functools.partial(reduce_kernel, shapes), out_shape=[jax.S...]
    reduce_scatter x1, waiting for transfers between devices: 97.6 us -> 0.01 us  [local(): lax.psum_scatter(grad_pairs.astype(jnp.bfloat16), 'ctx', scatter_dimensio...]
    psum x1 -> x0, waiting for transfers between devices: 86.9 us -> none  [local(): middle_own = lax.psum(middle_share, 'ctx').astype(jnp.float32)]
    reduce_scatter x2 -> x0, waiting for transfers between devices: 74.1 us -> none  [the longest x1 45.8 us: local(): lax.psum_scatter(middle_grads, 'wsh', scatter_dimension=0, tiled=True)]
    unnamed x10 -> x5, waiting for transfers between devices: 22.7 us -> 0.08 us
    unnamed x91 -> x118, local copies, waits for them, and re-layouts: 23.5 us -> 21.5 us
  transfers between devices with their start and end apart: 9 -> 5, of which waited for: 9 -> 4; matrix products, arithmetic and copies ran while one was open for 16% -> 21% of each run, Pallas kernels for 0% -> 26%
where the time goes in v2:
time: 453 us; the launch traced here: 444 us
  Pallas kernels  149 us (33%)
  local copies, waits for them, and re-layouts  84.7 us (19%)
  waiting for transfers between devices  83.6 us (18%)
  matrix products  79.3 us (18%)
  other arithmetic  30.6 us (7%)
  between operations  15.2 us (3%)
    pallas_call x2, Pallas kernels, reduce_all(): pl.pallas_call(functools.partial(reduce_kernel, shapes), out_shape=[jax.S...  149 us
    all_gather x1, waiting for transfers between devices, local(): all_pairs = lax.all_gather(pairs, 'ctx', axis=0, tiled=True)  46.3 us
    unnamed x118, local copies, waits for them, and re-layouts  21.5 us
    all_gather x1, waiting for transfers between devices, local(): first_all = lax.all_gather(first_pack, 'wsh', axis=0, tiled=True)  14.3 us
    dot_general x2, matrix products, exponents(): jnp.einsum('qsgrd,ksgd->sgrqk', queries, piece_keys, preferred_element_ty...  12.3 us
    all_gather x1, waiting for transfers between devices, local(): w_down = lax.all_gather(down_weight, 'wsh', axis=0, tiled=True)  11.8 us
    all_gather x1, waiting for transfers between devices, local(): middle_all = lax.all_gather(middle_pack, 'wsh', axis=0, tiled=True)  11.1 us
    dot_general x1, matrix products, backward_step(): jnp.einsum('sgrqk,qsgrd->ksgd', powers.astype(jnp.bfloat16), scaled, pref...  10.5 us
  transfers between devices with their start and end apart: 5, of which 4 were waited for; matrix products, arithmetic and copies ran while one was open for 21% of the time, Pallas kernels for 26%

profile of v2, /device:TPU:0, one launch (start us, length us, event | category | flops | bytes accessed | tf_op | source)
XLA Modules:
  0.0 443.7 jit_solution(10113673121929178245)
XLA Ops:
  10.7 2.4 copy.172
  16.7 14.3 %all-gather.5.cloned.1.call-done = bf16[576,962]{1,0:T(8,128)(2,1)} async-done(((bf16[144,962]{1,0:T(8,128)(2,1)}), bf16[576,962]{1,0:T(8,128)(2,1)}) %all-gather.5.cloned.1.call-update) | async-done | bytes 1108240 | tf_op jit(solution)/shard_map/all_gather | solution.py:227
  39.4 3.0 concatenate.66
  48.2 2.4 reshape.259
  50.6 2.8 subtract_convert_fusion.1
  56.3 46.3 %all-gather.7.cloned.1.call-done = bf16[2048,2,384]{0,2,1:T(8,128)(2,1)} async-done(((bf16[256,2,384]{0,2,1:T(8,128)(2,1)}), bf16[2048,2,384]{0,2,1:T(8,128)(2,1)}) %all-gather.7.cloned.1.call-update) | async-done | bytes 3145744 | tf_op jit(solution)/shard_map/all_gather | solution.py:303
  102.7 9.9 %while.26 = (s32[]{:T(128)}, f32[256,2,3,3,64]{0,4,3,2,1:T(8,128)S(1)}, f32[2,3,3,256]{3,2,1,0:T(4,128)S(1)}, s32[]{:T(128)}, bf16[2048,2,384]{0,2,1:T(8,128)(2,...) while((s32[]{:T(128)}, ...), condition=%wide.region_3.4_spmd.clone, body=%wide.region_1.3_spmd.clone.sunk | while | flops 1236829440 | bytes 46287040 | solution.py:55
  104.8 4.3 fusion.109
  109.2 3.4 fusion.110
  115.3 3.0 copy.186
  118.3 4.9 %fusion.56 = bf16[256,2,3,3,64]{4,3,2,1,0:T(4,128)(2,1)} fusion(f32[256,2,3,3,64]{4,3,2,1,0:T(4,128)} %copy.186, f32[256,2,3,3]{3,2,1,0:T(4,128)} %copy.185), kind=kLoop, calls=%fused_computation.120 | loop fusion | flops 589824 | bytes 1787904 | tf_op jit(solution)/shard_map/convert_element_type | solution.py:313
  123.2 2.9 reshape.260
  126.2 11.1 %all-gather.9.cloned.1.call-done = bf16[576,3648]{1,0:T(8,128)(2,1)} async-done(((bf16[144,3648]{1,0:T(8,128)(2,1)}), bf16[576,3648]{1,0:T(8,128)(2,1)}) %all-gather.9.cloned.1.call-update) | async-done | bytes 4202512 | tf_op jit(solution)/shard_map/all_gather | solution.py:236
  140.2 7.5 %fusion.33 = f32[512,3072]{1,0:T(8,128)} fusion(bf16[576,3648]{1,0:T(8,128)(2,1)} %all-gather.9.cloned.1.call-done, f32[512,576]{0,1:T(8,128)S(1)} %get-tuple-element.331, f32[576]{0:T(1024)S(1)} %get-tuple-element.259, f32[512]{0:T(512)S(1)} %fusion.51), kind=kOutput, calls=%fused_computation.54 | convolution fusion | flops 1812824064 | bytes 11014400 | tf_op jit(solution)/shard_map/dot_general | solution.py:316
  147.7 11.8 %all-gather.11.cloned.1.call-done = bf16[1536,576]{0,1:T(8,128)(2,1)} async-done(((bf16[384,576]{0,1:T(8,128)(2,1)}), bf16[1536,576]{0,1:T(8,128)(2,1)}) %all-gather.11.cloned.1.call-update) | async-done | bytes 1769488 | tf_op jit(solution)/shard_map/all_gather | solution.py:237
  159.5 5.6 %fusion.29 = (bf16[512,1536]{1,0:T(8,128)(2,1)S(1)}, bf16[512,1536]{1,0:T(8,128)(2,1)S(1)}, bf16[512,1536]{1,0:T(8,128)(2,1)}) fusion(f32[512,3072]{1,0:T(8,128)} %fusion.33, bf16[512,576]{1,0:T(8,128)(2,1)S(1)} %copy-done.21, bf16[1536,576]{0,1:T(8,128)(2,1)} %all-gather.11.cloned.1.call-done), kind=kOutput, calls=%fused_computation.40 | convolution fusion | flops 918552576 | bytes 13369344 | tf_op jit(solution)/shard_map/nd,fd->nf/dot_general | solution.py:324
  165.2 6.1 %multiply_reduce_fusion.1 = (bf16[576]{0:T(1024)(128)(2,1)}, f32[512]{0:T(512)S(1)}, f32[512,576]{0,1:T(8,128)S(1)}) fusion(f32[512,576]{0,1:T(8,128)S(1)} %copy-done.9, f32[512]{0:T(512)S(1)} %fusion.51, f32[576]{0:T(1024)S(1)} %get-tuple-element.259, bf16[576,3648]{1,0:T(8,128)(2,1)} %all-gather.9.cloned.1.call-done, ...), kind=kOutput, calls=%fused_computation.70 | convolution fusion | flops 1819999232 | bytes 9051520 | tf_op jit(solution)/shard_map/nf,df->nd/dot_general | solution.py:331
  172.7 3.0 fusion.45
  175.7 4.4 reshape.263
  180.1 6.3 %multiply_reduce_fusion = (f32[256,2,3,3]{3,2,1,0:T(4,128)S(1)}, bf16[256,2,3,3,64]{4,3,2,1,0:T(4,128)(2,1)}) fusion(f32[256,2,3,3,64]{4,3,2,1,0:T(4,128)} %reshape.263, f32[256,2,3,3,64]{4,3,2,1,0:T(4,128)} %copy.186, f32[256,2,3,3]{3,2,1,0:T(4,128)S(1)} %copy-done.12), kind=kLoop, calls=%fused_computation.44 | loop fusion | flops 1469952 | bytes 2985984 | tf_op jit(solution)/shard_map/reduce_sum | solution.py:341
  193.5 36.5 %while.27 = (s32[]{:T(128)}, f32[256,2,3,3,64]{0,4,3,2,1:T(8,128)S(1)}, bf16[2048,2,384]{0,2,1:T(8,128)(2,1)}, s32[]{:T(128)}, bf16[2048,2,384]{0,2,1:T(8,128)(2...) while((s32[]{:T(128)}, ...), condition=%wide.region_8.9_spmd.clone, body=%wide.region_7.8_spmd.clone.sunk | while | flops 3062433024 | bytes 103837944 | solution.py:55
  196.1 7.9 %fusion.121 = f32[2,3,1024,256,3]{3,2,4,1,0:T(8,128)} fusion(bf16[1024,2,3,64,1]{0,3,4,2,1:T(8,128)(2,1)S(1)} %bitcast.171, bf16[256,2,3,3,64]{0,4,3,2,1:T(8,128)(2,1)S(1)} %get-tuple-element.515), kind=kOutput, calls=%fused_computation.126.clone.1 | convolution fusion | flops 603979776 | bytes 20250624 | tf_op jit(solution)/shard_map/while/body/qsgrd,ksgd->sgrqk/dot_general | solution.py:284
  204.0 10.5 %fusion.124 = bf16[2,3,1024,64,1]{2,3,4,1,0:T(8,128)(2,1)} fusion(bf16[256,2,3,3,64]{0,4,3,2,1:T(8,128)(2,1)} %get-tuple-element.516, f32[2,3,1024,256,3]{3,2,4,1,0:T(8,128)} %fusion.121, pred[256,1024]{0,1:T(8,128)(4,1)} %broadcast_compare_fusion.5), kind=kOutput, calls=%fused_computation.21.clone.1 | convolution fusion | flops 618135552 | bytes 20512768 | tf_op jit(solution)/shard_map/while/body/sgrqk,qsgrd->ksgd/dot_general | solution.py:382
  214.5 9.1 %fusion.122 = bf16[2,3,3,256,1024]{3,4,2,1,0:T(8,128)(2,1)S(1)} fusion(f32[2,3,1024,256,3]{3,2,4,1,0:T(8,128)} %fusion.121, f32[2,3,3,256]{3,2,1,0:T(4,128)S(1)} %bitcast.188, pred[256,1024]{0,1:T(8,128)(4,1)} %broadcast_compare_fusion.5, bf16[1024,2,3,64,1]{0,3,4,2,1:T(8,128)(2,1)S(1)} %bitcast.177, bf16[256,2,3,3,64]{0,4,3,2,1:T(8,128)(2,1)} %get-tuple-element.516), kind=kOutput, calls=%fused_computation.18.clone.1 | convolution fusion | flops 627572736 | bytes 29968384 | tf_op jit(solution)/shard_map/while/body/qsgrd,ksgd->sgrqk/dot_general | solution.py:365
  225.5 2.9 bitcast_multiply_fusion.2
  231.7 3.1 fusion.35
  237.3 3.7 convolution_convert_fusion.1
  241.0 4.1 copy.209
  252.3 117.4 %shard_map.195 = (f32[144,1024]{1,0:T(8,128)S(1)}, f32[144,1024]{1,0:T(8,128)S(1)}, f32[144,1024]{1,0:T(8,128)S(1)}, f32[144,1024]{1,0:T(8,128)S(1)}, f32[384,576]{1,0:T(8,128)S(1)}) custom-call(bf16[2,2,144,1024]{3,2,1,0:T(8,128)(2,1)S(1)} %bitcast.170, bf16[2,2,144,1024]{3,2,1,0:T(8,128)(2,1)S(1)} %bitcast.169, bf16[2,2,144,1024]{3,2,1,0:T(8,128)(2,1)} %bitcast.180, ...), custom_call_target="tpu_custom_call" | custom-call | flops 12976128 | bytes 162201600 | tf_op jit(solution)/shard_map/pallas_call | solution.py:195
  377.5 3.7 subtract_convert_fusion
  394.9 2.5 multiply_reduce_fusion.2
  399.7 31.8 %shard_map.194 = f32[144,1024]{1,0:T(8,128)S(1)} custom-call(bf16[2,2,144,1024]{3,2,1,0:T(8,128)(2,1)S(1)} %maximum_maximum_fusion.refs_0_), custom_call_target="tpu_custom_call" | custom-call | flops 2359296 | bytes 29491200 | tf_op jit(solution)/shard_map/pallas_call | solution.py:195
  (222 shorter events, 85.3 us)
Async XLA Ops:
  7.2 5.9 %copy-start.23 = (bf16[256,2,576]{0,2,1:T(8,128)(2,1)S(1)}, bf16[256,2,576]{0,2,1:T(8,128)(2,1)}, u32[]{:S(2)}) copy-start(bf16[256,2,576]{0,2,1:T(8,128)(2,1)} %param.15) | copy-start | bytes 1769476
  7.2 23.8 %all-gather.5.cloned.1.call-start = ((), (), s32[]{:S(2)}) async-start(), calls=%async_computation.1 | async-start | bytes 1474560 | tf_op jit(solution)/shard_map/all_gather | solution.py:227
  10.7 91.9 %all-gather.7.cloned.1.call-start = ((), (), s32[]{:S(2)}) async-start(), calls=%async_computation.2 | async-start | bytes 3538944 | tf_op jit(solution)/shard_map/all_gather | solution.py:303
  14.2 18.2 %copy-start.47 = (f32[512]{0:T(512)}, f32[512]{0:T(512)S(1)}, u32[]{:S(2)}) copy-start(f32[512]{0:T(512)S(1)} %rsqrt.22) | copy-start | bytes 6148
  15.5 18.7 %copy-start.2 = (f32[512,576]{0,1:T(8,128)}, f32[512,576]{0,1:T(8,128)S(1)}, u32[]{:S(2)}) copy-start(f32[512,576]{0,1:T(8,128)S(1)} %copy.187) | copy-start | bytes 3538948
  16.7 33.9 %copy-start.18 = (f32[256,32]{1,0:T(8,128)}, f32[256,32]{1,0:T(8,128)S(1)}, u32[]{:S(2)}) copy-start(f32[256,32]{1,0:T(8,128)S(1)} %get-tuple-element.329) | copy-start | bytes 98308
  32.4 138.9 %copy-start.37 = (f32[576]{0:T(1024)}, f32[576]{0:T(1024)S(1)}, u32[]{:S(2)}) copy-start(f32[576]{0:T(1024)S(1)} %get-tuple-element.259) | copy-start | bytes 6916
  39.3 3.2 copy-start.29
  39.4 98.0 %all-gather.9.cloned.1.call-start = ((), (), s32[]{:S(2)}) async-start(), calls=%async_computation.3 | async-start | bytes 5345280 | tf_op jit(solution)/shard_map/all_gather | solution.py:236
  42.5 117.0 %all-gather.11.cloned.1.call-start = ((), (), s32[]{:S(2)}) async-start(), calls=%async_computation.4 | async-start | bytes 2211840 | tf_op jit(solution)/shard_map/all_gather | solution.py:237
  56.2 331.4 %reduce-scatter.2.cloned.1.call-start = ((), (), s32[]{:S(2)}) async-start(), calls=%async_computation.5 | async-start | bytes 3538944 | tf_op jit(solution)/shard_map/reduce_scatter | solution.py:405
  123.2 14.1 %copy-start.3 = (f32[512,576]{0,1:T(8,128)S(1)}, f32[512,576]{0,1:T(8,128)}, u32[]{:S(2)}) copy-start(f32[512,576]{0,1:T(8,128)} %copy-done.2) | copy-start | bytes 3538948
  126.2 13.0 %copy-start.15 = (bf16[512,576]{1,0:T(8,128)(2,1)}, bf16[512,576]{1,0:T(8,128)(2,1)S(1)}, u32[]{:S(2)}) copy-start(bf16[512,576]{1,0:T(8,128)(2,1)S(1)} %reshape.260) | copy-start | bytes 1769476
  139.2 32.1 %copy-start.39 = (f32[512]{0:T(512)}, f32[512]{0:T(512)S(1)}, u32[]{:S(2)}) copy-start(f32[512]{0:T(512)S(1)} %fusion.51) | copy-start | bytes 6148
  140.2 19.4 %copy-start.21 = (bf16[512,576]{1,0:T(8,128)(2,1)S(1)}, bf16[512,576]{1,0:T(8,128)(2,1)}, u32[]{:S(2)}) copy-start(bf16[512,576]{1,0:T(8,128)(2,1)} %copy-done.20) | copy-start | bytes 1769476
  147.7 17.5 %copy-start.9 = (f32[512,576]{0,1:T(8,128)S(1)}, f32[512,576]{0,1:T(8,128)}, u32[]{:S(2)}) copy-start(f32[512,576]{0,1:T(8,128)} %copy-done.8) | copy-start | bytes 3538948
  165.2 6.1 %copy-start.51 = (bf16[512,1536]{1,0:T(8,128)(2,1)}, bf16[512,1536]{1,0:T(8,128)(2,1)S(1)}, u32[]{:S(2)}) copy-start(bf16[512,1536]{1,0:T(8,128)(2,1)S(1)} %get-tuple-element.301) | copy-start | bytes 4718596
  165.2 6.1 %copy-start.53 = (bf16[512,1536]{1,0:T(8,128)(2,1)}, bf16[512,1536]{1,0:T(8,128)(2,1)S(1)}, u32[]{:S(2)}) copy-start(bf16[512,1536]{1,0:T(8,128)(2,1)S(1)} %get-tuple-element.302) | copy-start | bytes 4718596
  165.2 6.1 %copy-start.24 = (bf16[512,576]{0,1:T(8,128)(2,1)S(1)}, bf16[512,576]{0,1:T(8,128)(2,1)}, u32[]{:S(2)}) copy-start(bf16[512,576]{0,1:T(8,128)(2,1)} %copy.190) | copy-start | bytes 1769476
  175.7 4.4 copy-start.12
  180.1 6.3 %copy-start.17 = (f32[2,3,3,256]{2,1,0,3:T(4,128)S(1)}, f32[2,3,3,256]{2,1,0,3:T(4,128)}, u32[]{:S(2)}) copy-start(f32[2,3,3,256]{2,1,0,3:T(4,128)} %copy.193) | copy-start | bytes 55300
  186.4 2.7 copy-start.13
  225.5 3.0 copy-start.1
  230.0 5.1 %copy-start = (f32[256,2,3,3,64]{0,4,3,2,1:T(8,128)}, f32[256,2,3,3,64]{0,4,3,2,1:T(8,128)S(1)}, u32[]{:S(2)}) copy-start(f32[256,2,3,3,64]{0,4,3,2,1:T(8,128)S(1)} %get-tuple-element.110) | copy-start | bytes 3538948
  234.7 2.6 copy-start.22
  241.0 4.1 copy-start.49
  241.0 5.0 %copy-start.6 = (f32[512,576]{0,1:T(8,128)S(1)}, f32[512,576]{0,1:T(8,128)}, u32[]{:S(2)}) copy-start(f32[512,576]{0,1:T(8,128)} %copy-done.5) | copy-start | bytes 3538948
  241.0 5.0 %copy-start.16 = (bf16[512,576]{1,0:T(8,128)(2,1)S(1)}, bf16[512,576]{1,0:T(8,128)(2,1)}, u32[]{:S(2)}) copy-start(bf16[512,576]{1,0:T(8,128)(2,1)} %copy-done.15) | copy-start | bytes 1769476
  246.1 2.7 copy-start.54
  399.7 34.2 %copy-start.46 = (f32[512]{0:T(512)S(1)}, f32[512]{0:T(512)}, u32[]{:S(2)}) copy-start(f32[512]{0:T(512)} %copy-done.45) | copy-start | bytes 6148
  399.7 34.2 %copy-start.50 = (f32[512]{0:T(512)S(1)}, f32[512]{0:T(512)}, u32[]{:S(2)}) copy-start(f32[512]{0:T(512)} %get-tuple-element.256) | copy-start | bytes 6148
  399.7 34.2 %copy-start.7 = (f32[512,576]{0,1:T(8,128)S(1)}, f32[512,576]{0,1:T(8,128)}, u32[]{:S(2)}) copy-start(f32[512,576]{0,1:T(8,128)} %copy-done.5) | copy-start | bytes 3538948
  (28 other events, 47.4 us)
Sparse Core Ops, SparseCore 0:
  10.8 20.1 all-gather.4
  39.5 63.0 all-gather.6
  104.1 33.1 all-gather.8
  138.7 20.7 all-gather.10
  230.1 125.1 reduce-scatter.1
